TPU v7x, 32 devices: a whole 2x2x4 slice. The times are simulated.
32 devices in a mesh: dp: 8 (over z, x), tensor: 4 (over y, core).
Axes of the slice: x: 2, y: 2, z: 4, core: 2. Of those that a mesh axis runs over, the one named last changes fastest.
Arguments:
- hidden_in: bfloat16 [12288, 768], P('dp'), may hold values from -6 to 6
- token_mask: int32 [12288], P('dp'), may hold values from 0 to 1, as said below
- bucket: int32 [24], P('dp'), may hold values from 0 to 1, as said below
- positive: int32 [192], P('dp'), may hold values from 0 to 47, as said below
- qkv_weight: bfloat16 [3, 768, 768], P(None, None, 'tensor'), may hold values from -0.21875 to 0.21875
- qv_bias: bfloat16 [2, 768], P(None, 'tensor'), may hold values from -3 to 3
- out_weight: bfloat16 [768, 768], P('tensor'), may hold values from -1.25 to 1.25
- out_bias: bfloat16 [768], replicated, may hold values from -3 to 3
- norm1_gain: bfloat16 [768], replicated, may hold values from 0.25 to 1.75
- norm1_bias: bfloat16 [768], replicated, may hold values from -2 to 2
- ffn_in: bfloat16 [768, 3072], P(None, 'tensor'), may hold values from -0.21875 to 0.21875
- ffn_in_bias: bfloat16 [3072], P('tensor'), may hold values from -3 to 3
- ffn_out: bfloat16 [3072, 768], P('tensor'), may hold values from -0.15625 to 0.15625
- ffn_out_bias: bfloat16 [768], replicated, may hold values from -3 to 3
- norm2_gain: bfloat16 [768], replicated, may hold values from 0.25 to 1.75
- norm2_bias: bfloat16 [768], replicated, may hold values from -2 to 2
- upstream: bfloat16 [12288, 768], P('dp'), may hold values from -6 to 6
Outputs:
- layer_out: bfloat16 [12288, 768], P('dp')
- query_emb: bfloat16 [192, 768], P('dp')
- passage_emb: bfloat16 [48, 768], P('dp')
- loss: float32 [], replicated
- grad_in: float32 [12288, 768], P('dp')
- grad_qkv: float32 [3, 768, 768], P(None, None, 'tensor')
- grad_qv_bias: float32 [2, 768], P(None, 'tensor')
- grad_out_weight: float32 [768, 768], P('tensor')
- grad_out_bias: float32 [768], replicated
- grad_norm1_gain: float32 [768], replicated
- grad_norm1_bias: float32 [768], replicated
- grad_ffn_in: float32 [768, 3072], P(None, 'tensor')
- grad_ffn_in_bias: float32 [3072], P('tensor')
- grad_ffn_out: float32 [3072, 768], P('tensor')
- grad_ffn_out_bias: float32 [768], replicated
- grad_norm2_gain: float32 [768], replicated
- grad_norm2_bias: float32 [768], replicated
Inputs may be any that keep to these rules, and one draw needn't show every extreme that they name: `token_mask`: each block of 1536 rows holds 3 slots of 256 rows, then 24 queries of 32 rows. The real tokens of every sequence are a prefix of it: a bucket 1 slot has more than half of 256 real tokens, each half of a bucket 0 slot has from a quarter to a half of 256, a query has a quarter of 32 or more. The first slot has bucket 1 and the last slot bucket 0. `positive`: always a live candidate: 2 * s for some slot s, or 2 * s + 1 for a slot s of bucket 0.
All inputs are finite; a program needn't handle non-finite values.
Results may differ from a plain program's by a relative error of at most 0.015.
Values may be sent and summed in bfloat16 or wider, within the bound.
A program may use at most 128 MiB of HBM per device.

v0:
```python
from functools import partial
import math

import jax
import jax.numpy as jnp
from jax import lax
from jax.sharding import PartitionSpec as P

HEAD_DIM = 64
SLOT_LEN = 256
QRY_LEN = 32


NORM_EPS = 1e-12


def layer_norm(values, gain_row, bias_row):
    centre = values - jnp.mean(values, axis=-1, keepdims=True)
    spread = jnp.mean(centre * centre, axis=-1, keepdims=True)
    return centre * lax.rsqrt(spread + NORM_EPS) * gain_row + bias_row


def segment_ids(bucket, row_count, slot_count):
    row_index = jnp.arange(row_count, dtype=jnp.int32)
    slot_of = row_index // SLOT_LEN
    slot_place = row_index % SLOT_LEN
    slot_table = jnp.arange(slot_count, dtype=jnp.int32)
    slot_kind = jnp.sum(
        jnp.where(slot_of[:, None] == slot_table[None, :], bucket[None, :], 0), axis=1
    )
    in_slot = 2 * slot_of + jnp.where(slot_place >= SLOT_LEN // 2, 1 - slot_kind, 0)
    in_query = 2 * slot_count + (row_index - slot_count * SLOT_LEN) // QRY_LEN
    return jnp.where(row_index < slot_count * SLOT_LEN, in_slot, in_query)


def masked_scores(query_blk, key_blk, seg_blk, keep_blk):
    head_scale = 1.0 / math.sqrt(HEAD_DIM)
    raw_scores = (
        jnp.einsum("qhd,khd->hqk", query_blk, key_blk, preferred_element_type=jnp.float32)
        * head_scale
    )
    allowed = (seg_blk[:, None] == seg_blk[None, :]) & (keep_blk[None, :] == 1)
    return jnp.where(allowed[None], raw_scores, -1e30)


def attend_block(pieces):
    query_blk, key_blk, value_blk, seg_blk, keep_blk = pieces
    scores = masked_scores(query_blk, key_blk, seg_blk, keep_blk)
    peak = jnp.max(scores, axis=-1, keepdims=True)
    exp_scores = jnp.exp(scores - peak)
    exp_total = jnp.sum(exp_scores, axis=-1, keepdims=True)
    probs_low = (exp_scores / exp_total).astype(jnp.bfloat16)
    context = jnp.einsum("hqk,khd->qhd", probs_low, value_blk, preferred_element_type=jnp.float32)
    return (context.astype(jnp.bfloat16), (peak + jnp.log(exp_total))[..., 0])


def attend_back(pieces):
    query_blk, key_blk, value_blk, seg_blk, keep_blk, log_total, grad_context = pieces
    head_scale = 1.0 / math.sqrt(HEAD_DIM)
    scores = masked_scores(query_blk, key_blk, seg_blk, keep_blk)
    probs_full = jnp.exp(scores - log_total[..., None])
    grad_probs = jnp.einsum(
        "qhd,khd->hqk", grad_context, value_blk, preferred_element_type=jnp.float32
    )
    row_dot = jnp.sum(probs_full * grad_probs, axis=-1, keepdims=True)
    grad_scores = (probs_full * (grad_probs - row_dot)).astype(jnp.bfloat16)
    grad_query = (
        jnp.einsum("hqk,khd->qhd", grad_scores, key_blk, preferred_element_type=jnp.float32)
        * head_scale
    )
    grad_key = (
        jnp.einsum("hqk,qhd->khd", grad_scores, query_blk, preferred_element_type=jnp.float32)
        * head_scale
    )
    grad_value = jnp.einsum(
        "hqk,qhd->khd",
        probs_full.astype(jnp.bfloat16),
        grad_context,
        preferred_element_type=jnp.float32,
    )
    return (
        grad_query.astype(jnp.bfloat16),
        grad_key.astype(jnp.bfloat16),
        grad_value.astype(jnp.bfloat16),
    )


def local(
    hidden_in,
    token_mask,
    bucket,
    positive,
    qkv_weight,
    qv_bias,
    out_weight,
    out_bias,
    norm1_gain,
    norm1_bias,
    ffn_in,
    ffn_in_bias,
    ffn_out,
    ffn_out_bias,
    norm2_gain,
    norm2_bias,
    upstream,
):
    f32 = jnp.float32
    bf16 = jnp.bfloat16
    row_count, model_width = hidden_in.shape
    slot_count = bucket.shape[0]
    query_count = positive.shape[0]
    local_width = qkv_weight.shape[2]
    head_count = local_width // HEAD_DIM
    block_rows = 2 * SLOT_LEN
    block_count = row_count // block_rows
    slot_rows = slot_count * SLOT_LEN
    half_len = SLOT_LEN // 2
    loss_scale = 2.0 / math.sqrt(model_width)

    def split_heads(values):
        return values.reshape(block_count, block_rows, head_count, HEAD_DIM)

    segment = segment_ids(bucket, row_count, slot_count).reshape(block_count, block_rows)
    keep_rows = token_mask.reshape(block_count, block_rows)
    projected = jnp.einsum("rd,kde->kre", hidden_in, qkv_weight, preferred_element_type=f32)
    query_low = (projected[0] + qv_bias[0].astype(f32)).astype(bf16)
    key_low = projected[1].astype(bf16)
    value_low = (projected[2] + qv_bias[1].astype(f32)).astype(bf16)
    context, log_totals = lax.map(
        attend_block,
        (split_heads(query_low), split_heads(key_low), split_heads(value_low), segment, keep_rows),
    )
    context = context.reshape(row_count, local_width)
    attn_part = jnp.dot(context, out_weight, preferred_element_type=f32)
    attended = lax.psum(attn_part, "tensor") + out_bias.astype(f32)
    first_norm, norm1_back = jax.vjp(
        layer_norm, hidden_in.astype(f32) + attended, norm1_gain.astype(f32), norm1_bias.astype(f32)
    )
    first_low = first_norm.astype(bf16)
    inner = jnp.dot(first_low, ffn_in, preferred_element_type=f32) + ffn_in_bias.astype(f32)
    activated, gelu_back = jax.vjp(partial(jax.nn.gelu, approximate=False), inner)
    act_low = activated.astype(bf16)
    ffn_part = jnp.dot(act_low, ffn_out, preferred_element_type=f32)
    branch_out = lax.psum(ffn_part, "tensor") + ffn_out_bias.astype(f32)
    out_value, norm2_back = jax.vjp(
        layer_norm, first_norm + branch_out, norm2_gain.astype(f32), norm2_bias.astype(f32)
    )
    out_low = out_value.astype(bf16)
    passage_local = out_low[:slot_rows].reshape(slot_count, 2, half_len, model_width)[:, :, 0]
    passage_local = passage_local.reshape(2 * slot_count, model_width)
    query_local = out_low[slot_rows:].reshape(query_count, QRY_LEN, model_width)[:, 0]
    passages, slot_kinds = (
        lax.all_gather(passage_local, "dp", axis=0, tiled=True),
        lax.all_gather(bucket, "dp", axis=0, tiled=True),
    )
    cand_count = passages.shape[0]
    cand_valid = jnp.stack([slot_kinds >= 0, slot_kinds == 0], axis=1).reshape(cand_count)
    logits = jnp.einsum("qd,cd->qc", query_local, passages, preferred_element_type=f32) * loss_scale
    logits = jnp.where(cand_valid[None], logits, -1e30)
    peak = jnp.max(logits, axis=1, keepdims=True)
    log_total = peak + jnp.log(jnp.sum(jnp.exp(logits - peak), axis=1, keepdims=True))
    target = positive[:, None] == jnp.arange(cand_count, dtype=jnp.int32)[None, :]
    picked = jnp.sum(jnp.where(target, logits, 0.0), axis=1)
    loss_local = jnp.sum(log_total[:, 0] - picked)
    grad_logits = (jnp.exp(logits - log_total) - target.astype(f32)).astype(bf16)
    grad_query_emb = (
        jnp.einsum("qc,cd->qd", grad_logits, passages, preferred_element_type=f32) * loss_scale
    )
    grad_passages = (
        jnp.einsum("qc,qd->cd", grad_logits, query_local, preferred_element_type=f32) * loss_scale
    )
    grad_passage_local = lax.psum_scatter(grad_passages, "dp", scatter_dimension=0, tiled=True)
    grad_rows = upstream.astype(f32)
    grad_slots = grad_rows[:slot_rows].reshape(slot_count, 2, half_len, model_width)
    grad_slots = grad_slots.at[:, :, 0].add(grad_passage_local.reshape(slot_count, 2, model_width))
    grad_queries = grad_rows[slot_rows:].reshape(query_count, QRY_LEN, model_width)
    grad_queries = grad_queries.at[:, 0].add(grad_query_emb)
    grad_rows = jnp.concatenate(
        [
            grad_slots.reshape(slot_rows, model_width),
            grad_queries.reshape(row_count - slot_rows, model_width),
        ],
        axis=0,
    )
    grad_second, grad_gain_two, grad_bias_two = norm2_back(grad_rows)
    grad_branch = grad_second.astype(bf16)
    grad_ffn_out_bias = jnp.sum(grad_branch.astype(f32), axis=0)
    grad_ffn_out = jnp.einsum("rf,rd->fd", act_low, grad_branch, preferred_element_type=f32)
    grad_act = jnp.einsum("rd,fd->rf", grad_branch, ffn_out, preferred_element_type=f32)
    grad_inner = gelu_back(grad_act)[0].astype(bf16)
    grad_ffn_in_bias = jnp.sum(grad_inner.astype(f32), axis=0)
    grad_ffn_in = jnp.einsum("rd,rf->df", first_low, grad_inner, preferred_element_type=f32)
    first_part = jnp.einsum("rf,df->rd", grad_inner, ffn_in, preferred_element_type=f32)
    grad_first = grad_second + lax.psum(first_part, "tensor")
    ffn_sums = (
        grad_ffn_in,
        grad_ffn_in_bias,
        grad_ffn_out,
        grad_ffn_out_bias,
        grad_gain_two,
        grad_bias_two,
        loss_local,
    )
    grad_normed, grad_gain_one, grad_bias_one = norm1_back(grad_first)
    grad_attended = grad_normed.astype(bf16)
    grad_out_bias = jnp.sum(grad_attended.astype(f32), axis=0)
    grad_out_weight = jnp.einsum("re,rd->ed", context, grad_attended, preferred_element_type=f32)
    grad_context = jnp.einsum(
        "rd,ed->re", grad_attended, out_weight, preferred_element_type=f32
    ).astype(bf16)
    grad_query, grad_key, grad_value = lax.map(
        attend_back,
        (
            split_heads(query_low),
            split_heads(key_low),
            split_heads(value_low),
            segment,
            keep_rows,
            log_totals,
            split_heads(grad_context),
        ),
    )
    grad_proj = jnp.stack(
        [
            grad_query.reshape(row_count, local_width),
            grad_key.reshape(row_count, local_width),
            grad_value.reshape(row_count, local_width),
        ]
    )
    grad_qv_bias = jnp.stack(
        [jnp.sum(grad_proj[0].astype(f32), axis=0), jnp.sum(grad_proj[2].astype(f32), axis=0)]
    )
    grad_qkv = jnp.einsum("rd,kre->kde", hidden_in, grad_proj, preferred_element_type=f32)
    input_part = jnp.einsum("kre,kde->rd", grad_proj, qkv_weight, preferred_element_type=f32)
    grad_in = grad_normed + lax.psum(input_part.astype(jnp.bfloat16), "tensor").astype(jnp.float32)
    every_sum = lax.psum(
        (
            grad_qkv,
            grad_qv_bias,
            grad_out_weight,
            grad_out_bias,
            grad_gain_one,
            grad_bias_one,
            grad_ffn_in,
            grad_ffn_in_bias,
            grad_ffn_out,
            grad_ffn_out_bias,
            grad_gain_two,
            grad_bias_two,
            loss_local,
        ),
        "dp",
    )
    attn_sums = every_sum[:6]
    ffn_sums = every_sum[6:]
    loss_mean = ffn_sums[6] / (query_count * lax.axis_size("dp"))
    return (
        out_low,
        query_local,
        passage_local,
        loss_mean,
        grad_in,
        attn_sums[0],
        attn_sums[1],
        attn_sums[2],
        attn_sums[3],
        attn_sums[4],
        attn_sums[5],
        ffn_sums[0],
        ffn_sums[1],
        ffn_sums[2],
        ffn_sums[3],
        ffn_sums[4],
        ffn_sums[5],
    )


def solution(mesh):
    placed = (
        P("dp", None),
        P("dp"),
        P("dp"),
        P("dp"),
        P(None, None, "tensor"),
        P(None, "tensor"),
        P("tensor", None),
        P(),
        P(),
        P(),
        P(None, "tensor"),
        P("tensor"),
        P("tensor", None),
        P(),
        P(),
        P(),
        P("dp", None),
    )
    return jax.shard_map(
        local,
        mesh=mesh,
        in_specs=placed,
        out_specs=(
            P("dp", None),
            P("dp", None),
            P("dp", None),
            P(),
            P("dp", None),
            P(None, None, "tensor"),
            P(None, "tensor"),
            P("tensor", None),
            P(),
            P(),
            P(),
            P(None, "tensor"),
            P("tensor"),
            P("tensor", None),
            P(),
            P(),
            P(),
        ),
        check_vma=False,
    )
```

profile of v0, /device:TPU:0, one launch (start us, length us, event | category | flops | bytes accessed | tf_op | source)
XLA Modules:
  0.0 841.6 jit_solution(2481379935586764478)
XLA Ops:
  7.2 3.6 convolution_bitcast_fusion
  13.3 1.9 squeeze.43
  15.9 2.0 squeeze.44
  18.4 2.1 convert_element_type.130
  22.9 12.4 %while.28 = (s32[]{:T(128)}, bf16[3,512,3,64]{1,3,2,0:T(8,128)(2,1)}, f32[3,3,512]{2,1,0:T(4,128)}, bf16[3,512,3,64]{1,3,2,0:T(8,128)(2,1)S(1)}, s32[3,512]{1,0:...) while((s32[]{:T(128)}, ...), condition=%wide.region_4.5_spmd, body=%wide.region_1.4_spmd.sunk | while | flops 211385344 | bytes 11339365 | solution.py:129
  25.2 1.8 fusion.151
  29.4 1.8 fusion.151
  33.5 1.8 fusion.151
  35.3 2.0 copy.99
  38.3 3.0 fusion.98
  44.5 93.8 %all-reduce.11.cloned.1.call-done = f32[1536,768]{1,0:T(8,128)} async-done(((f32[1536,768]{1,0:T(8,128)}), f32[1536,768]{1,0:T(8,128)}) %all-reduce.11.cloned.1.call-update) | async-done | bytes 4718608 | tf_op jit(solution)/shard_map/psum | solution.py:135
  138.3 3.0 fusion.92
  144.2 13.1 %multiply_convert_fusion.1 = (bf16[1536,768]{1,0:T(8,128)(2,1)S(1)}, f32[1536,768]{1,0:T(8,128)}, f32[1536,768]{1,0:T(8,128)}) fusion(f32[768]{0:T(1024)S(1)} %copy-done.57, bf16[1536,768]{1,0:T(8,128)(2,1)S(1)} %fusion.61, bf16[768,768]{1,0:T(8,128)(2,1)S(1)} %copy-done), kind=kOutput, calls=%fused_computation.83 | convolution fusion | flops 1889796096 | bytes 15338496 | tf_op jit(solution)/shard_map/dot_general | solution.py:140
  158.8 4.2 fusion.99
  165.1 11.3 %all-reduce = s32[24]{0:T(128)S(1)} all-reduce(s32[24]{0:T(128)S(1)} %dynamic-update-slice.6), channel_id=1, replica_groups=mesh['dp'=8,'tensor'=4] {'dp'}, use_global_device_ids=true, to_apply=%add | all-reduce | flops 24 | bytes 192
  179.0 3.4 fusion.94
  183.7 73.6 %all-reduce.13.cloned.1.call-done = f32[1536,768]{1,0:T(8,128)} async-done(((f32[1536,768]{1,0:T(8,128)}), f32[1536,768]{1,0:T(8,128)}) %all-reduce.13.cloned.1.call-update) | async-done | bytes 4718608 | tf_op jit(solution)/shard_map/psum | solution.py:144
  257.4 4.8 fusion.90
  268.3 32.8 %all-gather = bf16[8,6,768]{2,1,0:T(8,128)(2,1)} all-gather(bf16[1,6,768]{2,1,0:T(8,128)(2,1)} %reshape.402), channel_id=1, replica_groups=mesh['dp'=8,'tensor'=4] {'dp'}, dimensions={0}, use_global_device_ids=true | all-gather | bytes 82944 | tf_op jit(solution)/shard_map/all_gather | solution.py:153
  306.9 1.6 convolution_multiply_fusion.2
  308.5 24.1 %fusion = f32[8,768]{1,0:T(8,128)} fusion(f32[48,768]{1,0:T(8,128)} %convolution_multiply_fusion.2), kind=kCustom, calls=%all-reduce-scatter | all-reduce-scatter fusion | flops 49153 | bytes 172544
  334.0 1.9 collective-permute-start
  335.9 2.4 collective-permute-start.1
  340.2 2.8 scatter-add.9
  343.0 4.3 concatenate.8
  350.5 1.6 scatter-add.6
  352.1 5.8 multiply_reduce_fusion.1
  358.5 2.9 fusion.89
  361.5 2.2 copy-done.4
  364.8 4.1 convert_reduce_fusion.1
  370.3 4.3 fusion.100
  374.7 5.1 fusion.103
  379.8 85.7 %all-reduce.15.cloned.1.call-done = f32[1536,768]{1,0:T(8,128)} async-done(((f32[1536,768]{1,0:T(8,128)}), f32[1536,768]{1,0:T(8,128)}) %all-reduce.15.cloned.1.call-update) | async-done | bytes 4718608 | tf_op jit(solution)/shard_map/psum | solution.py:194
  465.6 7.2 multiply_reduce_fusion.2
  472.8 3.8 fusion.88
  476.7 2.1 copy-done.3
  486.5 26.6 %while.29 = (s32[]{:T(128)}, bf16[3,512,3,64]{1,3,2,0:T(8,128)(2,1)S(1)}, bf16[3,512,3,64]{1,3,2,0:T(8,128)(2,1)}, bf16[3,512,3,64]{1,3,2,0:T(8,128)(2,1)}, bf16...) while((s32[]{:T(128)}, ...), condition=%wide.region_24.25_spmd, body=%wide.region_22.24_spmd.sunk | while | flops 511409152 | bytes 26130560 | solution.py:211
  519.3 1.7 stack_reshape.11
  521.9 1.9 constant_dynamic-update-slice_fusion
  523.8 5.4 bitcast_convert_fusion
  529.3 5.3 fusion.102
  536.1 2.7 fusion.65
  541.4 1.9 reduce_sum.267
  545.6 38.4 %all-reduce.3 = (f32[]{:T(128)}, f32[2,192]{1,0:T(2,128)}, f32[768]{0:T(1024)}, f32[768]{0:T(1024)}, f32[768]{0:T(1024)}, /*index=5*/f32[768]{0:T(1024)}, f32[768]{0:T(1024)}, f32[768]{0:T(1024)}, f32[768]{0:T(1024)}) all-reduce(f32[]{:T(128)} %get-tuple-element.295, ...), channel_id=1, replica_groups=mesh['dp'=8,'tensor'=4] {'dp'}, use_global_device_ids=true, to_apply=%region_15.16 | all-reduce | flops 5761 | bytes 46088 | tf_op jit(solution)/shard_map/psum | solution.py:236
  585.2 5.8 convert_add_fusion
  591.0 235.0 %all-reduce.19.cloned.1.call-done = (f32[3,768,192]{1,2,0:T(8,128)}, f32[192,768]{1,0:T(8,128)}, f32[768,768]{1,0:T(8,128)}, f32[768,768]{1,0:T(8,128)}) async-done(((f32[3,768,192]{1,2,0:T(8,128)}, f32[192,768]{1,0:T(8,128)}, f32[768,768]{1,0:T(8,128)}, f32[768,768]{1,0:T(8,128)}), (f32[3,768,192]{1,2,0:T(8,128)}, f32[192,768]{1,0:T(8,128)}, f32[768,768]{1,0:T(8,128)}, ...) | async-done | bytes 7077904 | tf_op jit(solution)/shard_map/psum | solution.py:236
  826.0 2.9 copy.165
  829.0 1.9 copy.166
  (303 shorter events, 98.4 us)
Async XLA Ops:
  7.2 136.9 %copy-start = (bf16[768,768]{1,0:T(8,128)(2,1)S(1)}, bf16[768,768]{1,0:T(8,128)(2,1)}, u32[]{:S(2)}) copy-start(bf16[768,768]{1,0:T(8,128)(2,1)} %param.35) | copy-start | bytes 3538948
  7.2 131.0 %all-reduce.11.cloned.1.call-start = ((), (), s32[]{:S(2)}) async-start(), calls=%async_computation | async-start | bytes 9437184 | tf_op jit(solution)/shard_map/psum | solution.py:135
  15.8 5.9 copy-start.67
  15.9 6.1 copy-start.55
  22.8 15.4 %copy-start.29 = (bf16[192,768]{1,0:T(8,128)(2,1)S(1)}, bf16[192,768]{1,0:T(8,128)(2,1)}, u32[]{:S(2)}) copy-start(bf16[192,768]{1,0:T(8,128)(2,1)} %param.31) | copy-start | bytes 884740
  35.2 6.0 copy-start.9
  35.2 6.0 copy-start.11
  35.2 6.0 copy-start.19
  35.2 6.0 copy-start.39
  35.3 6.0 copy-start.40
  41.3 96.9 %copy-start.24 = (bf16[1536,768]{1,0:T(8,128)(2,1)S(1)}, bf16[1536,768]{1,0:T(8,128)(2,1)}, u32[]{:S(2)}) copy-start(bf16[1536,768]{1,0:T(8,128)(2,1)} %param.25) | copy-start | bytes 7077892
  41.4 216.0 %all-reduce.13.cloned.1.call-start = ((), (), s32[]{:S(2)}) async-start(), calls=%async_computation.1 | async-start | bytes 9437184 | tf_op jit(solution)/shard_map/psum | solution.py:144
  144.2 13.2 %copy-start.13 = (bf16[1536,768]{1,0:T(8,128)(2,1)}, bf16[1536,768]{1,0:T(8,128)(2,1)S(1)}, u32[]{:S(2)}) copy-start(bf16[1536,768]{1,0:T(8,128)(2,1)S(1)} %fusion.61) | copy-start | bytes 7077892
  144.2 14.6 %copy-start.69 = (bf16[768,768]{1,0:T(8,128)(2,1)S(1)}, bf16[768,768]{1,0:T(8,128)(2,1)}, u32[]{:S(2)}) copy-start(bf16[768,768]{1,0:T(8,128)(2,1)} %param.37) | copy-start | bytes 3538948
  163.0 13.5 %copy-start.63 = (bf16[768]{0:T(1024)(128)(2,1)S(1)}, bf16[768]{0:T(1024)(128)(2,1)}, u32[]{:S(2)}) copy-start(bf16[768]{0:T(1024)(128)(2,1)} %param.38) | copy-start | bytes 4612
  163.0 14.1 %copy-start.64 = (bf16[768]{0:T(1024)(128)(2,1)S(1)}, bf16[768]{0:T(1024)(128)(2,1)}, u32[]{:S(2)}) copy-start(bf16[768]{0:T(1024)(128)(2,1)} %param.39) | copy-start | bytes 4612
  163.0 14.7 %copy-start.65 = (bf16[768]{0:T(1024)(128)(2,1)S(1)}, bf16[768]{0:T(1024)(128)(2,1)}, u32[]{:S(2)}) copy-start(bf16[768]{0:T(1024)(128)(2,1)} %param.40) | copy-start | bytes 4612
  163.0 302.5 %all-reduce.15.cloned.1.call-start = ((), (), s32[]{:S(2)}) async-start(), calls=%async_computation.2 | async-start | bytes 9437184 | tf_op jit(solution)/shard_map/psum | solution.py:194
  334.0 9.0 %collective-permute-start = (f32[8,768]{1,0:T(8,128)}, f32[8,768]{1,0:T(8,128)}, u32[]{:S(2)}, u32[]{:S(2)}) collective-permute-start(f32[8,768]{1,0:T(8,128)} %fusion), channel_id=1, source_target_pairs={{0,4},{4,8},{8,12},{12,16},{16,20},{20,24},{24,28},{1,5},{5,9},{9,... | collective-permute-start | bytes 73736
  335.9 7.1 collective-permute-start.1
  348.7 9.2 %slice-start = ((s8[4718592]{0:T(1024)(128)(4,1)}), s8[524288]{0:T(1024)(128)(4,1)S(1)}, s32[]{:S(2)}) async-start(s8[4718592]{0:T(1024)(128)(4,1)} %bitcast.190), calls=%async_computation.5 | async-start | bytes 1048576
  352.1 5.8 copy-start.46
  352.1 5.8 slice-start.1
  352.1 5.8 copy-start.6
  352.1 6.4 copy-start.8
  352.1 6.4 copy-start.32
  352.1 6.4 copy-start.36
  352.1 6.4 copy-start.50
  357.9 6.8 slice-start.2
  357.9 6.8 slice-start.4
  358.5 6.2 slice-start.3
  358.5 6.2 slice-start.5
  374.6 210.6 %all-reduce.17.cloned.1.call-start = ((), (), s32[]{:S(2)}) async-start(), calls=%async_computation.3 | async-start | bytes 4718592 | tf_op jit(solution)/shard_map/psum | solution.py:235
  379.8 93.0 %copy-start.44 = (f32[1536]{0:T(1024)S(1)}, f32[1536]{0:T(1024)}, u32[]{:S(2)}) copy-start(f32[1536]{0:T(1024)} %copy-done.43) | copy-start | bytes 18436
  379.8 93.0 %copy-start.38 = (f32[768]{0:T(1024)S(1)}, f32[768]{0:T(1024)}, u32[]{:S(2)}) copy-start(f32[768]{0:T(1024)} %convert_element_type.132) | copy-start | bytes 9220
  481.3 5.2 copy-start.10
  481.3 5.2 copy-start.12
  513.1 7.9 copy-start.16
  523.8 5.5 copy-start.14
  529.2 296.8 %all-reduce.19.cloned.1.call-start = ((), (), s32[]{:S(2)}) async-start(), calls=%async_computation.4 | async-start | bytes 14155776 | tf_op jit(solution)/shard_map/psum | solution.py:236
  529.3 5.3 copy-start.18
  529.3 5.3 copy-start.27
  529.3 6.8 copy-start.25
  529.3 6.8 copy-start.34
  539.5 6.0 copy-start.52
  540.6 5.0 copy-start.53
  540.6 44.6 %copy-start.48 = (f32[1536]{0:T(1024)S(1)}, f32[1536]{0:T(1024)}, u32[]{:S(2)}) copy-start(f32[1536]{0:T(1024)} %copy-done.47) | copy-start | bytes 18436
  826.0 6.3 copy-start.22
  (36 other events, 73.7 us)
Sparse Core Ops, SparseCore 0:
  41.5 96.7 all-reduce.10
  163.2 94.1 all-reduce.12
  374.8 90.7 all-reduce.14
  529.4 55.8 all-reduce.16
  590.1 235.8 all-reduce.18
where the time goes:
time: 850 us; the launch traced here: 842 us
  waiting for transfers between devices  489 us (58%)
  blocking collectives  107 us (13%)
  matrix products  81.8 us (10%)
  local copies, waits for them, and re-layouts  79.9 us (9%)
  other arithmetic  61.5 us (7%)
  between operations  18 us (2%)
    psum x1, waiting for transfers between devices, local(): lax.psum((grad_qkv, grad_qv_bias, grad_out_weight, grad_out_bias, grad_ga...  235 us
    psum x1, waiting for transfers between devices, local(): attended = lax.psum(attn_part, 'tensor') + out_bias.astype(f32)  93.8 us
    psum x1, waiting for transfers between devices, local(): grad_first = grad_second + lax.psum(first_part, 'tensor')  85.7 us
    psum x1, waiting for transfers between devices, local(): branch_out = lax.psum(ffn_part, 'tensor') + ffn_out_bias.astype(f32)  73.6 us
    psum x1, blocking collectives, local(): lax.psum((grad_qkv, grad_qv_bias, grad_out_weight, grad_out_bias, grad_ga...  38.4 us
    unnamed x171, local copies, waits for them, and re-layouts  35.7 us
    unnamed x2, blocking collectives  35.5 us
    all_gather x1, blocking collectives, local(): lax.all_gather(passage_local, 'dp', axis=0, tiled=True)  32.8 us
  transfers between devices with their start and end apart: 7, of which 5 were waited for; matrix products, arithmetic and copies ran while one was open for 5% of the time, Pallas kernels for 0%

commit v1 on v0

v1 whole, which is shorter than its diff:
```python
import math
from types import SimpleNamespace

import jax
import jax.numpy as jnp
from jax import lax
from jax.experimental import pallas as pl
from jax.experimental.pallas import tpu as pltpu
from jax.sharding import PartitionSpec as P

f32 = jnp.float32
bf16 = jnp.bfloat16
MESH = pl.DeviceIdType.MESH

HEAD_DIM = 64
SLOT_LEN = 256
QRY_LEN = 32
NORM_EPS = 1e-12
BLK = 256
PIECE = 64
RING = 8
DEAD = -1e30


def dot(a, b):
    return lax.dot_general(a, b, (((1,), (0,)), ((), ())), preferred_element_type=f32)


def dot_t(a, b):
    return lax.dot_general(a, b, (((1,), (1,)), ((), ())), preferred_element_type=f32)


def dot_l(a, b):
    return lax.dot_general(a, b, (((0,), (0,)), ((), ())), preferred_element_type=f32)


def loop(n, body, lo=0):
    def step(i, carry):
        body(i)
        return carry

    lax.fori_loop(lo, n, step, 0)


def layer_kernel(n_dp, dims, names, *refs):
    R = SimpleNamespace(**dict(zip(names, refs)))
    rows, width, slots, queries, local_width = dims
    blocks = rows // BLK
    heads = local_width // HEAD_DIM
    groups = n_dp // RING
    cands = 8 * n_dp
    loss_scale = 2.0 / math.sqrt(width)
    quarter = width
    own = blocks * PIECE
    part_rows = own // 2

    dp = lax.axis_index("dp")
    t = lax.axis_index("tensor")
    y = lax.div(t, 2)
    c = lax.rem(t, 2)
    t1 = 2 * y + (1 - c)
    t2 = 2 * (1 - y) + c
    t3 = 2 * (1 - y) + (1 - c)
    core = (dp, t1)
    ypeer = (dp, t2)
    mates = ((dp, t1), (dp, t2), (dp, t3))

    group = lax.div(dp, RING)
    place = lax.rem(dp, RING)

    def place_of(r):
        return jnp.where(r < 4, 2 * r, 2 * (7 - r) + 1)

    r = jnp.where(lax.rem(place, 2) == 0, lax.div(place, 2), 7 - lax.div(place, 2))
    ring_to = (
        (group * RING + place_of(lax.rem(r + 1, RING)), t),
        (group * RING + place_of(lax.rem(r + RING - 1, RING)), t),
    )

    def dp_at(k):
        return lax.rem(dp + k, n_dp)

    (S_SHARE, S_WCORE, S_WRING, S_WON, S_BIAS, S_CORE0, S_Y0, S_CORE1, S_Y1, S_X1, S_FIRST, S_DF, S_DA, S_OUT, S_MAIL,
     S_BACK, S_VEC, S_TSUM, S_RING, S_GATHER, S_LOCAL, S_GLOCAL, S_GCORE, S_OUTL) = range(24)

    def cp(src, dst, kind, rsem, dev):
        return pltpu.make_async_remote_copy(
            src_ref=src, dst_ref=dst, send_sem=R.ss.at[kind], recv_sem=rsem, device_id=dev, device_id_type=MESH
        )

    def arrived(ref, rsem):
        cp(ref, ref, S_SHARE, rsem, core).wait_recv()

    def sent(ref, kind):
        cp(ref, ref, kind, R.wc_r.at[0], core).wait_send()

    loads = [
        pltpu.make_async_copy(R.wqkv_in, R.wqkv, R.load_sem.at[0]),
        pltpu.make_async_copy(R.hid_in, R.hid, R.load_sem.at[1]),
        pltpu.make_async_copy(R.wo_in, R.wo, R.load_sem.at[2]),
        pltpu.make_async_copy(R.w1, R.wf1.at[t], R.load_sem.at[3]),
        pltpu.make_async_copy(R.w2, R.wf2.at[t], R.load_sem.at[4]),
        pltpu.make_async_copy(R.upstream.at[:, t], R.up, R.load_sem.at[5]),
    ]
    for one in loads:
        one.start()

    barrier = pltpu.get_barrier_semaphore()
    for mate in mates:
        pl.semaphore_signal(barrier, inc=1, device_id=mate, device_id_type=MESH)

    def greet(k):
        pl.semaphore_signal(barrier, inc=1, device_id=(dp_at(k), t), device_id_type=MESH)

    loop(n_dp, greet, 1)
    pl.semaphore_wait(barrier, 3 + n_dp - 1)

    share = quarter // RING
    half = share // 2
    wfs = (R.wf1, R.wf2)
    wins = (R.w1, R.w2)
    rb = R.rb

    def unit(chunk, sub):
        return pl.ds(pl.multiple_of(chunk * share + sub * half, half), half)

    def from_here(d, s):
        return lax.rem(r - s + 2 * RING, RING) if d == 0 else lax.rem(r + s + 2 * RING, RING)

    def w_share(k):
        at = pl.ds(pl.multiple_of(r * share, share), share)
        return cp(wins[k].at[at], wfs[k].at[t, at], S_SHARE, R.wy_r.at[k], ypeer)

    def w_send(k, at, d, idx):
        ref = wfs[k].at[t2, at]
        cp(ref, ref, S_WRING, R.wr_r.at[idx], ring_to[d]).start()

    def w_on(k, at):
        ref = wfs[k].at[t2, at]
        cp(ref, ref, S_WON, R.wf_r.at[0], core).start()

    def w_start():
        for k in range(2):
            at = pl.ds(pl.multiple_of(r * share, share), share)
            arrived(wfs[k].at[t2, at], R.wy_r.at[k])
            for d in range(2):
                w_send(k, unit(r, d), d, 0)
                w_send(k, unit(r, 1 - d), d, 4)
            w_on(k, at)

    def w_lead(s):
        arrived(rb.at[0:2, :, 0], R.wr_r.at[s - 1])
        for k in range(2):
            for d in range(2):
                at = unit(from_here(d, s), d)
                if s < 4:
                    w_send(k, at, d, s)
                w_on(k, at)

    def w_trail(s):
        arrived(rb.at[0:2, :, 0], R.wr_r.at[3 + s])
        for k in range(2):
            for d in range(2):
                at = unit(from_here(d, s), 1 - d)
                if s < 3:
                    w_send(k, at, d, 4 + s)
                w_on(k, at)

    for k in range(2):
        w_share(k).start()
    for k in range(2):
        cp(wins[k], wfs[k].at[t], S_WCORE, R.wc_r.at[0], core).start()
    R.bias1[t] = jnp.broadcast_to(R.b1[...].astype(f32).reshape(1, quarter), (8, quarter))
    for mate in mates:
        cp(R.bias1.at[t], R.bias1.at[t], S_BIAS, R.bi_r.at[0], mate).start()

    part = R.part
    keep, send1, got1, send2, got2 = R.keep, R.send1, R.got1, R.send2, R.got2

    def rs0(e, i):
        for yy in range(2):
            mine = pl.ds(pl.multiple_of((2 * yy + c) * PIECE, PIECE), PIECE)
            other = pl.ds(pl.multiple_of((2 * yy + 1 - c) * PIECE, PIECE), PIECE)
            keep[i, yy] = part[mine].astype(bf16)
            send1[i, yy] = part[other].astype(bf16)
        cp(send1.at[i], got1.at[i], (S_CORE0, S_CORE1)[e], R.rc_r.at[e, i], core).start()

    def rs1(i):
        arrived(got1.at[i], R.rc_r.at[0, i])
        send2[i, 0] = (keep[i, 1 - y].astype(f32) + got1[i, 1 - y].astype(f32)).astype(bf16)
        cp(send2.at[i, 0], got2.at[i, 0], S_Y0, R.ry_r.at[0, i], ypeer).start()

    def rs2(i):
        arrived(got2.at[i, 0], R.ry_r.at[0, i])
        return keep[i, y].astype(f32) + got1[i, y].astype(f32) + got2[i, 0].astype(f32)

    def ag0(mine, kind, ysem, csem):
        cp(mine, mine, kind, ysem, ypeer).start()
        cp(mine, mine, kind, csem, core).start()

    def ag1(theirs, kind, ysem, csem):
        arrived(theirs, ysem)
        cp(theirs, theirs, kind, csem, core).start()

    def ag2(first, second, csem):
        arrived(first, csem)

    hid, wqkv, wo = R.hid, R.wqkv, R.wo
    lane = lax.broadcasted_iota(jnp.int32, (1, local_width), 1)
    head_f = [jnp.where(lax.shift_right_logical(lane, 6) == h, 1.0, 0.0).astype(f32) for h in range(heads)]
    head_b = [m.astype(bf16) for m in head_f]
    q_bias = R.qv_bias[0:1].astype(f32)
    v_bias = R.qv_bias[1:2].astype(f32)
    head_scale = 1.0 / math.sqrt(HEAD_DIM)

    def allowed_of(i):
        row = lax.broadcasted_iota(jnp.int32, (BLK, 1), 0)
        col = lax.broadcasted_iota(jnp.int32, (1, BLK), 1)
        split = 1 - R.bucket[jnp.minimum(i, slots - 1)]
        is_query = jnp.where(i >= slots, 1, 0)

        def seg(at):
            in_query = lax.shift_right_logical(at, 5)
            in_slot = lax.shift_right_logical(at, 7) * split
            return in_query * is_query + in_slot * (1 - is_query)

        return (seg(row) == seg(col)) & (R.mask[blk(i)].reshape(1, BLK) == 1)

    def blk(i):
        return pl.ds(pl.multiple_of(i * BLK, BLK), BLK)

    def attend(i):
        h_in = hid[blk(i)]
        q = (dot_t(h_in, wqkv[0]) + q_bias).astype(bf16)
        k = dot_t(h_in, wqkv[1]).astype(bf16)
        v = (dot_t(h_in, wqkv[2]) + v_bias).astype(bf16)
        R.q[blk(i)] = q
        R.k[blk(i)] = k
        R.v[blk(i)] = v
        allowed = allowed_of(i)
        context = jnp.zeros((BLK, local_width), f32)
        for h in range(heads):
            s = jnp.where(allowed, dot_t(q * head_b[h], k) * head_scale, DEAD)
            e = jnp.exp(s - jnp.max(s, axis=-1, keepdims=True))
            p = (e / jnp.sum(e, axis=-1, keepdims=True)).astype(bf16)
            R.pb[i, h] = p
            context = context + dot(p, v) * head_f[h]
        low = context.astype(bf16)
        R.ctx[blk(i)] = low
        part[...] = dot(low, wo[...])

    def norm_fwd(v, gain, bias):
        centre = v - jnp.mean(v, axis=-1, keepdims=True)
        rstd = lax.rsqrt(jnp.mean(centre * centre, axis=-1, keepdims=True) + NORM_EPS)
        n = centre * rstd
        return n, rstd, n * gain + bias

    def norm_bwd(dy, n, rstd, gain):
        e = dy * gain
        return (e - jnp.mean(e, axis=-1, keepdims=True) - n * jnp.mean(e * n, axis=-1, keepdims=True)) * rstd

    def vec_of(ref):
        return ref[...].astype(f32).reshape(1, width)

    vec = SimpleNamespace(
        ob=vec_of(R.ob), g1=vec_of(R.g1), n1b=vec_of(R.n1b), fb=vec_of(R.fb), g2=vec_of(R.g2), n2b=vec_of(R.n2b)
    )
    x1 = R.x1
    h1, n1, n2 = R.h1, R.n1, R.n2
    rstd1, rstd2 = R.rstd1, R.rstd2

    def own_rows(i):
        return pl.ds(pl.multiple_of(i * BLK + t * PIECE, PIECE), PIECE)

    def part_at(b, i):
        return pl.ds(pl.multiple_of(b * part_rows + i * 32, 32), 32)

    def first_norm(i):
        v = hid[own_rows(i)].astype(f32) + rs2(i) + vec.ob
        n, rstd, out = norm_fwd(v, vec.g1, vec.n1b)
        wide_rstd = jnp.broadcast_to(rstd, (PIECE, 128)).reshape(2, 2, 16, 128)
        n = n.reshape(2, 2, 16, width)
        low = out.astype(bf16)
        out = out.reshape(2, 2, 16, width)
        low4 = low.reshape(2, 2, 16, width)
        for b in range(2):
            n1[part_at(b, i)] = n[:, b].reshape(32, width)
            rstd1[part_at(b, i)] = wide_rstd[:, b].reshape(32, 128)
            h1[part_at(b, i)] = out[:, b].reshape(32, width)
            R.x1_own[part_at(b, i)] = low4[:, b].reshape(32, width)
        x1[i, t] = low
        ag0(x1.at[i, t], S_X1, R.gy_r.at[i], R.gc_r.at[i])

    def at_step(s, jobs):
        for i, job in jobs.items():
            pl.when(s == i)(job)

    def fwd_step(s):
        attend(s)
        rs0(0, s)

        @pl.when(s >= 1)
        def _():
            rs1(s - 1)

        at_step(s, {3: w_start})

        @pl.when(s >= 3)
        def _():
            first_norm(s - 3)

    for one in loads[:3]:
        one.wait()
    loop(blocks, fwd_step)
    rs1(blocks - 1)
    w_lead(1)
    first_norm(blocks - 3)
    w_trail(1)
    first_norm(blocks - 2)
    first_norm(blocks - 1)
    w_lead(2)

    for one in loads[3:]:
        one.wait()
    arrived(R.bias1.at[0:3], R.bi_r.at[0])
    arrived(R.wf1.at[0:2], R.wc_r.at[0])
    act, slope = R.act, R.slope

    def gelu(u):
        cdf = 0.5 * (1.0 + lax.erf(u * (1.0 / math.sqrt(2.0))))
        pdf = jnp.exp(-0.5 * u * u) * (1.0 / math.sqrt(2.0 * math.pi))
        return (u * cdf).astype(bf16), (cdf + u * pdf).astype(bf16)

    wide = R.wide
    wide[...] = jnp.zeros((own, width), f32)

    def own_fwd(j):
        q = jnp.where(j == 0, t, jnp.where(j == 1, t1, jnp.where(j == 2, t2, t3)))
        u = dot(R.x1_own[...], wfs[0][q]) + R.bias1[q, 0:1]
        a, sl = gelu(u)
        R.slope_own[q] = sl
        wide[...] += dot(a, wfs[1][q])

    def quarter_fwd(i):
        ag1(x1.at[i, t2], S_X1, R.gy_r.at[i], R.gc_r.at[i])
        arrived(x1.at[i, 0:2], R.gc_r.at[i])
        u = dot(x1[i].reshape(BLK, width), wfs[0][t]) + R.bias1[t, 0:1]
        a, sl = gelu(u)
        act[i] = a.reshape(4, 2, 2, 16, width)
        slope[i] = sl.reshape(4, 2, 2, 16, width)

    def middle(s):
        @pl.when(s < 2)
        def _():
            own_fwd(s)

        @pl.when((s >= 2) & (s < blocks + 2))
        def _():
            quarter_fwd(s - 2)

        at_step(s, {0: lambda: w_trail(2), 1: lambda: w_lead(3), 3: lambda: w_trail(3), 5: lambda: w_lead(4)})

        @pl.when(s >= blocks + 2)
        def _():
            @pl.when(s == blocks + 3)
            def _():
                arrived(R.wf1.at[0:2], R.wf_r.at[0])

            own_fwd(s - blocks)

    loop(blocks + 4, middle)

    low_out = R.low

    def second_norm(j):
        at = pl.ds(pl.multiple_of(j * PIECE, PIECE), PIECE)
        n, rstd, out = norm_fwd(h1[at] + wide[at] + vec.fb, vec.g2, vec.n2b)
        n2[at] = n
        rstd2[at] = jnp.broadcast_to(rstd, (PIECE, 128))
        h1[at] = out
        b = lax.div(j, blocks // 2)
        i = 2 * lax.rem(j, blocks // 2)
        low_out[pl.ds(i, 2), :, b] = out.astype(bf16).reshape(2, 2, 16, width)

    loop(blocks, second_norm)

    firsts = R.firsts
    stage = R.stage
    stage[...] = jnp.zeros((16, width), f32)
    for b in range(blocks - slots):
        for k in range(2):
            at = (slots + b) * 32 + 16 * k
            stage[2 * b + k : 2 * b + k + 1] = h1[at : at + 1]
    for s in range(slots):
        stage[6 + s : 7 + s] = h1[32 * s : 32 * s + 1]
    firsts[t] = stage[...].astype(bf16)
    for mate in mates:
        cp(firsts.at[t], firsts.at[t], S_FIRST, R.fi_r.at[0], mate).start()

    sums = R.sums
    sums[...] = jnp.zeros((16, width), f32)
    adds = R.adds
    up, dv2, df, da = R.up, R.n2, R.df, R.da
    dv1 = R.h1

    def colsum(v):
        return jnp.sum(v, axis=0, keepdims=True)

    def second_back(b):
        def one(i):
            at = part_at(b, i)
            dy = up[i, :, b].reshape(32, width).astype(f32)
            if b == 0:
                row = lax.broadcasted_iota(jnp.int32, (32, 1), 0)
                dy = dy + jnp.where(row == 0, adds[i, 0:1], 0.0) + jnp.where(row == 16, adds[i, 1:2], 0.0)
            n = n2[at]
            sums[0:1] += colsum(dy * n)
            sums[1:2] += colsum(dy)
            dv = norm_bwd(dy, n, rstd2[at][:, 0:1], vec.g2)
            dv2[at] = dv
            low = dv.astype(bf16)
            sums[2:3] += colsum(low.astype(f32))
            df[i, t, :, b] = low.reshape(2, 16, width)

        loop(blocks, one)
        ag0(df.at[:, t, :, b], S_DF, R.fy_r.at[b], R.fc_r.at[b])

    def own_bwd(b):
        at = pl.ds(b * part_rows, part_rows)
        wide[at] = dv2[at]

        def one(q):
            dg = dot_t(df[:, t, :, b].reshape(part_rows, width), wfs[1][q])
            du = (dg * R.slope_own[q, at].astype(f32)).astype(bf16)
            wide[at] += dot_t(du, wfs[0][q])

        loop(4, one)

        def first_back(i):
            at = part_at(b, i)
            dy = wide[at]
            n = n1[at]
            sums[3:4] += colsum(dy * n)
            sums[4:5] += colsum(dy)
            dv = norm_bwd(dy, n, rstd1[at][:, 0:1], vec.g1)
            dv1[at] = dv
            low = dv.astype(bf16)
            sums[5:6] += colsum(low.astype(f32))
            da[i, t, :, b] = low.reshape(2, 16, width)

        loop(blocks, first_back)
        ag0(da.at[:, t, :, b], S_DA, R.ay_r.at[b], R.ac_r.at[b])

    def df_on(b):
        ag1(df.at[:, t2, :, b], S_DF, R.fy_r.at[b], R.fc_r.at[b])

    def da_on(b):
        ag1(da.at[:, t2, :, b], S_DA, R.ay_r.at[b], R.ac_r.at[b])

    du_all = slope

    def quarter_bwd(b):
        arrived(df.at[:, 0:2, :, b], R.fc_r.at[b])

        def one(j):
            at = pl.ds(2 * j, 2)
            dg = dot_t(df[at, :, :, b].reshape(BLK, width), wfs[1][t])
            du = (dg * slope[at, :, :, b].reshape(BLK, width).astype(f32)).astype(bf16)
            sums[8:9] += colsum(du.astype(f32))
            du_all[at, :, :, b] = du.reshape(2, 4, 2, 16, width)

        loop(blocks // 2, one)

    second_back(1)

    arrived(firsts.at[0:3], R.fi_r.at[0])
    hw = width // 2
    pack = R.pack
    pack[...] = jnp.zeros((16, hw + 128), f32)
    cand_rows = [firsts[0].astype(f32), firsts[2].astype(f32)]
    for k in range(2):
        pack[3 * k : 3 * k + 3, 0:hw] = cand_rows[k][6:9, 0:hw]
        pack[8 + 3 * k : 11 + 3 * k, 0:hw] = cand_rows[k][6:9, hw:width]
    for s in range(slots):
        pack[3 + s : 4 + s, hw : hw + 128] = jnp.zeros((1, 128), f32) + R.bucket[s].astype(f32)
    pack[6:8, hw : hw + 128] = jnp.ones((2, 128), f32)
    mail = R.mail
    mail[dp] = pack[...].astype(bf16)
    loop(n_dp, lambda k: cp(mail.at[dp], mail.at[dp], S_MAIL, R.dp_r.at[0], (dp_at(k), t)).start(), 1)

    qe = R.qe
    qe[...] = jnp.zeros(qe.shape, f32)
    for tt in range(4):
        qe[8 * tt : 8 * tt + 6, 0:width] = firsts[tt].astype(f32)[0:6]
    lane_e = lax.broadcasted_iota(jnp.int32, (32, 128), 1)
    qe[:, width : width + 128] = jnp.where(lane_e == 0, DEAD, 0.0)
    row_q = lax.broadcasted_iota(jnp.int32, (32, 1), 0)
    target_at = jnp.full((32, 1), -1, jnp.int32)
    for tt in range(4):
        for b in range(blocks - slots):
            for k in range(2):
                pos = R.positive[b * 8 + tt * 2 + k]
                slot = lax.div(pos, 2)
                at = lax.div(slot, slots) * 8 + lax.rem(pos, 2) * 3 + lax.rem(slot, slots)
                target_at = jnp.where(row_q == 8 * tt + 2 * b + k, at, target_at)

    own_bwd(1)

    arrived(mail.at[1:], R.dp_r.at[0])
    pe = R.pe

    def unpack(n):
        got = mail[n].astype(f32)
        at = pl.ds(pl.multiple_of(n * 8, 8), 8)
        pe[at, 0:hw] = got[0:8, 0:hw]
        pe[at, hw:width] = got[8:16, 0:hw]
        pe[at, width : width + 128] = got[0:8, hw : hw + 128]

    loop(n_dp, unpack)
    pe_low = pe[...].astype(bf16)
    qe_low = qe[...].astype(bf16)
    z = dot_t(qe_low, pe_low) * loss_scale
    peak = jnp.max(z, axis=1, keepdims=True)
    total = peak + jnp.log(jnp.sum(jnp.exp(z - peak), axis=1, keepdims=True))
    target = lax.broadcasted_iota(jnp.int32, (32, cands), 1) == target_at
    live = target_at >= 0
    picked = jnp.sum(jnp.where(target, z, 0.0), axis=1, keepdims=True)
    ce = jnp.where(live, total - picked, 0.0)
    loss = jnp.sum(ce, axis=0, keepdims=True)
    dz = jnp.where(live, jnp.exp(z - total) - jnp.where(target, 1.0, 0.0), 0.0).astype(bf16)
    dqe = R.dqe
    dqe[...] = dot(dz, pe_low[:, 0:width]) * loss_scale
    dpe = R.dpe
    dpe[...] = (dot_l(dz, qe_low[:, 0:width]) * loss_scale).reshape(n_dp, 8, width)
    back = R.back

    @pl.when(c == 0)
    def _():
        loop(n_dp, lambda k: cp(dpe.at[dp_at(k)], back.at[dp], S_BACK, R.dp_r.at[1], (dp_at(k), t)).start(), 1)

    back[dp] = dpe[dp]

    df_on(1)
    da_on(1)
    quarter_bwd(1)

    @pl.when(c == 0)
    def _():
        arrived(back.at[1:], R.dp_r.at[1])
        stage[0:8] = back[0]

        def add(n):
            stage[0:8] += back[n]

        loop(n_dp, add, 1)

    mine_q = dqe[pl.ds(pl.multiple_of(t * 8, 8), 8)]
    is_c0 = jnp.where(c == 0, 1.0, 0.0).astype(f32)
    adds[...] = jnp.zeros(adds.shape, f32)
    for s in range(slots):
        adds[s, 0:1] = jnp.where(y == 0, stage[s : s + 1], stage[3 + s : 4 + s]) * is_c0
    for b in range(blocks - slots):
        adds[slots + b, 0:2] = mine_q[2 * b : 2 * b + 2]
    second_back(0)
    own_bwd(0)

    out = R.layer_out
    out_own = pltpu.make_async_copy(low_out, out.at[:, t], R.ss.at[S_OUTL])
    out_own.start()
    cp(low_out, out.at[:, t], S_OUT, R.lo_r.at[0], ypeer).start()
    cp(low_out, out.at[:, t], S_OUT, R.lo_r.at[1], core).start()

    sums[6:7] = jnp.where(t == 0, loss, 0.0) + jnp.zeros((1, width), f32)
    tsum = R.tsum
    tsum[t] = sums[0:8]
    for mate in mates:
        cp(tsum.at[t], tsum.at[t], S_TSUM, R.ts_r.at[0], mate).start()
    df_on(0)
    quarter_bwd(0)

    grads = (R.ga1, R.ga2, R.ga3)
    outs = (R.o1, R.o2, R.o3)

    def to_owner(d, s):
        return from_here(1 - d, 4 - s)

    def ring_send(k, d, src, idx):
        cp(src, rb.at[k, d, idx], S_RING, R.rr_r.at[k, idx], ring_to[d]).start()

    def ring_start(k):
        for d in range(2):
            ring_send(k, d, grads[k].at[unit(to_owner(d, 0), d)], 0)
            ring_send(k, d, grads[k].at[unit(to_owner(d, 1), 1 - d)], 4)

    def ring_add(k, s, lead):
        idx = s - 1 if lead else s + 2
        arrived(rb.at[k, :, idx], R.rr_r.at[k, idx])
        for d in range(2):
            slot = rb.at[k, d, idx]
            mine = grads[k][unit(to_owner(d, s), d if lead else 1 - d)]
            slot[...] = (slot[...].astype(f32) + mine.astype(f32)).astype(bf16)
            ring_send(k, d, slot, idx + 1)

    def gather_send(k, d, src, at, idx):
        cp(src, outs[k].at[at], S_GATHER, R.rg_r.at[k, idx], ring_to[d]).start()

    def ring_turn(k):
        for idx in (3, 6):
            arrived(rb.at[k, :, idx], R.rr_r.at[k, idx])
        for a in range(2):
            mine = grads[k][unit(r, a)].astype(f32)
            rb[k, a, 3] = (rb[k, a, 3].astype(f32) + rb[k, 1 - a, 6].astype(f32) + mine).astype(bf16)
        if groups > 1:

            def swap(a, g):
                at = (k * 2 + a) * (groups - 1) + g - 1
                dev = (lax.rem(group + g, groups) * RING + place, t)
                return pltpu.make_async_remote_copy(
                    src_ref=rb.at[k, a, 3], dst_ref=R.gb.at[at], send_sem=R.gr_s.at[at], recv_sem=R.gr_r.at[at],
                    device_id=dev, device_id_type=MESH,
                )

            both = [(a, g) for a in range(2) for g in range(1, groups)]
            for a, g in both:
                swap(a, g).start()
            for a, g in both:
                swap(a, g).wait()
            for a in range(2):
                tot = rb[k, a, 3].astype(f32)
                for g in range(1, groups):
                    tot = tot + R.gb[(k * 2 + a) * (groups - 1) + g - 1].astype(f32)
                rb[k, a, 3] = tot.astype(bf16)
        for d in range(2):
            gather_send(k, d, rb.at[k, d, 3], unit(r, d), 0)
            gather_send(k, d, rb.at[k, 1 - d, 3], unit(r, 1 - d), 4)
        for a in range(2):
            pltpu.make_async_copy(rb.at[k, a, 3], outs[k].at[unit(r, a)], R.ss.at[S_LOCAL]).start()

    def gather_on(k, s, lead):
        idx = s - 1 if lead else s + 3
        arrived(rb.at[k, :, 0], R.rg_r.at[k, idx])
        if s < (4 if lead else 3):
            for d in range(2):
                at = unit(from_here(d, s), d if lead else 1 - d)
                gather_send(k, d, outs[k].at[at], at, idx + 1)

    def ring_jobs(k):
        return [
            lambda: ring_add(k, 1, True), lambda: ring_add(k, 2, False), lambda: ring_add(k, 2, True),
            lambda: ring_add(k, 3, False), lambda: ring_add(k, 3, True), lambda: ring_turn(k),
            lambda: gather_on(k, 1, True), lambda: gather_on(k, 1, False), lambda: gather_on(k, 2, True),
            lambda: gather_on(k, 2, False), lambda: gather_on(k, 3, True), lambda: gather_on(k, 3, False),
            lambda: gather_on(k, 4, True),
        ]

    tile = BLK

    def grad2(j):
        at = pl.ds(pl.multiple_of(j * tile, tile), tile)
        grads[1][at] = dot_l(act[..., at].reshape(rows, tile), df[...].reshape(rows, width)).astype(bf16)

    loop(quarter // tile, grad2)
    ring_start(1)
    da_on(0)

    def grad1(j):
        at = pl.ds(pl.multiple_of(j * tile, tile), tile)
        grads[0][:, at] = dot_l(x1[...].reshape(rows, width), du_all[..., at].reshape(rows, tile)).astype(bf16)

    loop(quarter // tile, grad1)
    ring_start(0)

    dq_all, dk_all, dv_all = R.q, R.k, R.v

    def attend_back(i):
        da_i = da[i].reshape(BLK, width)
        dc = dot_t(da_i, wo[...]).astype(bf16)
        q = R.q[blk(i)]
        k = R.k[blk(i)]
        v = R.v[blk(i)]
        dq = jnp.zeros((BLK, local_width), f32)
        dk = jnp.zeros((BLK, local_width), f32)
        dv = jnp.zeros((BLK, local_width), f32)
        for h in range(heads):
            dch = dc * head_b[h]
            p = R.pb[i, h]
            pf = p.astype(f32)
            dp_h = dot_t(dch, v)
            ds = (pf * (dp_h - jnp.sum(pf * dp_h, axis=-1, keepdims=True))).astype(bf16)
            dq = dq + dot(ds, k) * head_f[h]
            dk = dk + dot_l(ds, q * head_b[h])
            dv = dv + dot_l(p, dch)
        dq = (dq * head_scale).astype(bf16)
        dk = (dk * head_scale).astype(bf16)
        dv = dv.astype(bf16)
        dq_all[blk(i)] = dq
        dk_all[blk(i)] = dk
        dv_all[blk(i)] = dv
        sums[9:10, 0:local_width] += colsum(dq.astype(f32))
        sums[10:11, 0:local_width] += colsum(dv.astype(f32))
        part[...] = dot(dq, wqkv[0]) + dot(dk, wqkv[1]) + dot(dv, wqkv[2])

    gin = R.grad_in

    def gin1(i):
        arrived(got1.at[i], R.rc_r.at[1, i])
        mine = [dv1[part_at(b, i)].reshape(2, 16, width) for b in range(2)]
        mine = jnp.stack(mine, axis=1).reshape(PIECE, width)
        for yy in range(2):
            has = jnp.where(y == yy, 1.0, 0.0).astype(f32)
            send2[i, yy] = (keep[i, yy].astype(f32) + got1[i, yy].astype(f32) + mine * has).astype(bf16)
        cp(send2.at[i], got2.at[i], S_Y1, R.ry_r.at[1, i], ypeer).start()

    def gin2(i):
        arrived(got2.at[i], R.ry_r.at[1, i])
        for yy in range(2):
            got2[i, yy] = (send2[i, yy].astype(f32) + got2[i, yy].astype(f32)).astype(bf16)
            dst = gin.at[i, 2 * yy + c]
            pltpu.make_async_copy(got2.at[i, yy], dst, R.ss.at[S_GLOCAL]).start()
            cp(got2.at[i, yy], dst, S_GCORE, R.go_r.at[0], core).start()

    sent(send1, S_CORE0)
    sent(send2.at[:, 0], S_Y0)
    for b in range(2):
        arrived(da.at[:, 0:2, :, b], R.ac_r.at[b])

    jobs1, jobs0, jobs2 = ring_jobs(1), ring_jobs(0), ring_jobs(2)
    n_early = blocks

    def back_step(s):
        attend_back(s)
        rs0(1, s)

        @pl.when(s >= 1)
        def _():
            gin1(s - 1)

        at_step(s, dict(enumerate(jobs1[:n_early])))
        at_step(s, dict(enumerate(jobs0[:n_early])))

        @pl.when(s >= 3)
        def _():
            gin2(s - 3)

    loop(blocks, back_step)

    grads[2][0:local_width] = dot_l(dq_all[...], hid[...]).astype(bf16)
    grads[2][local_width : 2 * local_width] = dot_l(dk_all[...], hid[...]).astype(bf16)
    grads[2][2 * local_width : 3 * local_width] = dot_l(dv_all[...], hid[...]).astype(bf16)
    grads[2][3 * local_width : 4 * local_width] = dot_l(R.ctx[...], da[...].reshape(rows, width)).astype(bf16)
    ring_start(2)

    arrived(tsum.at[0:3], R.ts_r.at[0])
    sums[0:8] = tsum[0] + tsum[1] + tsum[2] + tsum[3]
    loss_low = sums[6:7].astype(bf16).astype(f32)
    sums[7:8] = sums[6:7] - loss_low
    vmail = R.vmail
    vmail[dp] = sums[...].astype(bf16)
    loop(n_dp, lambda k: cp(vmail.at[dp], vmail.at[dp], S_VEC, R.dp_r.at[2], (dp_at(k), t)).start(), 1)

    extra = [lambda: gin1(blocks - 1)] + [lambda i=i: gin2(i) for i in range(blocks - 3, blocks)]
    late1, late0 = jobs1[n_early:], jobs0[n_early:]
    for i in range(max(len(jobs2), len(late1), len(extra))):
        for jobs in (late1, late0, jobs2, extra):
            if i < len(jobs):
                jobs[i]()

    arrived(vmail.at[1:], R.dp_r.at[2])
    sums[...] = vmail[0].astype(f32)

    def vec_add(n):
        sums[...] += vmail[n].astype(f32)

    loop(n_dp, vec_add, 1)
    R.vec_out[...] = sums[...]
    piece = x1.at[:, 0]
    arrived(piece, R.lo_r.at[0])
    cp(out.at[:, t2], out.at[:, t2], S_OUT, R.lo_r.at[1], core).start()
    arrived(x1.at[:, 0:2], R.lo_r.at[1])
    arrived(send1, R.go_r.at[0])

    out_own.wait()
    sent(x1.at[0, 0:3], S_SHARE)
    sent(R.wf1.at[0:2], S_WCORE)
    sent(rb.at[0:2], S_WRING)
    sent(R.wf1.at[0:2], S_WON)
    sent(R.bias1.at[0:3], S_BIAS)
    sent(send1, S_CORE1)
    sent(send2, S_Y1)
    for kind in (S_X1, S_DF, S_DA, S_OUT):
        sent(x1.at[:, 0:3], kind)
    sent(firsts.at[0:3], S_FIRST)
    sent(mail.at[1:], S_MAIL)
    sent(vmail.at[1:], S_VEC)
    sent(tsum.at[0:3], S_TSUM)

    @pl.when(c == 0)
    def _():
        sent(back.at[1:], S_BACK)

    sent(rb, S_RING)
    sent(rb, S_GATHER)
    sent(send1, S_GCORE)
    pltpu.make_async_copy(rb.at[0, 0, 0:6], rb.at[0, 0, 0:6], R.ss.at[S_LOCAL]).wait()
    pltpu.make_async_copy(send1, send1, R.ss.at[S_GLOCAL]).wait()


def run_layer(n_dp, ins, dims):
    rows, width, slots, queries, local_width = dims
    blocks = rows // BLK
    heads = local_width // HEAD_DIM
    own = blocks * PIECE
    groups = n_dp // RING
    share = width // RING // 2
    dma = pltpu.SemaphoreType.DMA
    vm = pltpu.VMEM
    any_ = pl.BlockSpec(memory_space=pl.ANY)
    vmem = pl.BlockSpec(memory_space=pltpu.VMEM)
    smem = pl.BlockSpec(memory_space=pltpu.SMEM)
    ins_at = dict(
        hid_in=any_, mask=vmem, bucket=smem, positive=smem, wqkv_in=any_, qv_bias=vmem, wo_in=any_, ob=vmem, g1=vmem,
        n1b=vmem, w1=any_, b1=vmem, w2=any_, fb=vmem, g2=vmem, n2b=vmem, upstream=any_,
    )
    pieces = (blocks, 4, 2, 2, 16, width)
    pairs = (blocks, 2, PIECE, width)
    outs = dict(
        layer_out=(any_, pieces, bf16),
        grad_in=(any_, (blocks, 4, PIECE, width), bf16),
        o1=(any_, (width, width), bf16),
        o2=(any_, (width, width), bf16),
        o3=(any_, (width, width), bf16),
        vec_out=(vmem, (16, width), f32),
    )
    scratch = dict(
        hid=vm((rows, width), bf16),
        wqkv=vm((3, local_width, width), bf16),
        wo=vm((local_width, width), bf16),
        wf1=vm((4, width, width), bf16),
        wf2=vm((4, width, width), bf16),
        up=vm((blocks, 2, 2, 16, width), bf16),
        bias1=vm((4, 8, width), f32),
        part=vm((BLK, width), f32),
        keep=vm(pairs, bf16),
        send1=vm(pairs, bf16),
        got1=vm(pairs, bf16),
        send2=vm(pairs, bf16),
        got2=vm(pairs, bf16),
        q=vm((rows, local_width), bf16),
        k=vm((rows, local_width), bf16),
        v=vm((rows, local_width), bf16),
        ctx=vm((rows, local_width), bf16),
        pb=vm((blocks, heads, BLK, BLK), bf16),
        x1=vm((blocks, 4, PIECE, width), bf16),
        x1_own=vm((own, width), bf16),
        h1=vm((own, width), f32),
        n1=vm((own, width), f32),
        n2=vm((own, width), f32),
        rstd1=vm((own, 128), f32),
        rstd2=vm((own, 128), f32),
        act=vm(pieces, bf16),
        slope=vm(pieces, bf16),
        wide=vm((own, width), f32),
        slope_own=vm((4, own, width), bf16),
        low=vm((blocks, 2, 2, 16, width), bf16),
        firsts=vm((4, 16, width), bf16),
        stage=vm((16, width), f32),
        adds=vm((blocks, 8, width), f32),
        pack=vm((16, width // 2 + 128), f32),
        mail=vm((n_dp, 16, width // 2 + 128), bf16),
        qe=vm((32, width + 128), f32),
        pe=vm((n_dp * 8, width + 128), f32),
        dqe=vm((32, width), f32),
        dpe=vm((n_dp, 8, width), f32),
        back=vm((n_dp, 8, width), f32),
        sums=vm((16, width), f32),
        tsum=vm((4, 8, width), f32),
        vmail=vm((n_dp, 16, width), bf16),
        df=vm(pieces, bf16),
        da=vm(pieces, bf16),
        ga1=vm((width, width), bf16),
        ga2=vm((width, width), bf16),
        ga3=vm((width, width), bf16),
        rb=vm((3, 2, RING - 1, share, width), bf16),
        load_sem=dma((6,)),
        ss=dma((24,)),
        wc_r=dma((1,)), wy_r=dma((2,)), wf_r=dma((1,)), wr_r=dma((7,)), bi_r=dma((1,)),
        rc_r=dma((2, blocks)), ry_r=dma((2, blocks)),
        gy_r=dma((blocks,)), gc_r=dma((blocks,)),
        fy_r=dma((2,)), fc_r=dma((2,)), ay_r=dma((2,)), ac_r=dma((2,)),
        fi_r=dma((1,)), lo_r=dma((2,)), dp_r=dma((3,)), ts_r=dma((1,)),
        rr_r=dma((3, 7)), rg_r=dma((3, 7)), go_r=dma((1,)),
    )
    if groups > 1:
        n = 6 * (groups - 1)
        scratch.update(gb=vm((n, share, width), bf16), gr_s=dma((n,)), gr_r=dma((n,)))
    names = [*ins_at, *outs, *scratch]

    def kernel(*refs):
        layer_kernel(n_dp, dims, names, *refs)

    return pl.pallas_call(
        kernel,
        name="layer",
        out_shape=[jax.ShapeDtypeStruct(shape, kind) for _, shape, kind in outs.values()],
        in_specs=list(ins_at.values()),
        out_specs=[spec for spec, _, _ in outs.values()],
        scratch_shapes=list(scratch.values()),
        compiler_params=pltpu.CompilerParams(
            collective_id=0, has_side_effects=True, vmem_limit_bytes=64 * 2**20
        ),
    )(*[ins[n] for n in ins_at])


def local(
    hidden_in, token_mask, bucket, positive, qkv_weight, qv_bias, out_weight, out_bias, norm1_gain, norm1_bias,
    ffn_in, ffn_in_bias, ffn_out, ffn_out_bias, norm2_gain, norm2_bias, upstream,
):
    rows, width = hidden_in.shape
    blocks = rows // BLK
    slots = bucket.shape[0]
    queries = positive.shape[0]
    local_width = qkv_weight.shape[2]
    n_dp = lax.axis_size("dp")
    ins = dict(
        hid_in=hidden_in, mask=token_mask, bucket=bucket, positive=positive, wqkv_in=qkv_weight.transpose(0, 2, 1),
        qv_bias=qv_bias, wo_in=out_weight, ob=out_bias, g1=norm1_gain, n1b=norm1_bias, w1=ffn_in, b1=ffn_in_bias,
        w2=ffn_out, fb=ffn_out_bias, g2=norm2_gain, n2b=norm2_bias,
        upstream=upstream.reshape(blocks, 4, 2, 2, 16, width),
    )
    lout, gin, o1, o2, o3, sums = run_layer(n_dp, ins, (rows, width, slots, queries, local_width))
    lout = lout.reshape(rows, width)
    slot_rows = slots * SLOT_LEN
    passage = lout[:slot_rows].reshape(2 * slots, SLOT_LEN // 2, width)[:, 0]
    query = lout[slot_rows:].reshape(queries, QRY_LEN, width)[:, 0]
    qkv = o3[: 3 * local_width].reshape(3, local_width, width)
    loss = (sums[6, 0] + sums[7, 0]) / (queries * n_dp)
    return (
        lout, query, passage, loss, gin.reshape(rows, width).astype(f32),
        qkv.transpose(0, 2, 1).astype(f32), sums[9:11, :local_width], o3[3 * local_width :].astype(f32),
        sums[5], sums[3], sums[4], o1.astype(f32), sums[8], o2.astype(f32), sums[2], sums[0], sums[1],
    )


def solution(mesh):
    one, two = P("dp"), P("dp", None)
    col, row = P(None, "tensor"), P("tensor", None)
    return jax.shard_map(
        local,
        mesh=mesh,
        in_specs=(
            two, one, one, one, P(None, None, "tensor"), col, row, P(), P(), P(), col, P("tensor"), row, P(), P(), P(),
            two,
        ),
        out_specs=(
            two, two, two, P(), two, P(None, None, "tensor"), col, row, P(), P(), P(), col, P("tensor"), row, P(), P(),
            P(),
        ),
        check_vma=False,
    )
```

time: 850 us -> 197 us (0.23)
  waiting for transfers between devices: 489 us -> 0 us
  Pallas kernels: 0 us -> 176 us
  blocking collectives: 107 us -> 0 us
  matrix products: 81.8 us -> 0 us
  local copies, waits for them, and re-layouts: 79.9 us -> 10.1 us
  other arithmetic: 61.5 us -> 8.05 us
  between operations: 18 us -> 3.14 us
    psum x5 -> x0, waiting for transfers between devices: 489 us -> none  [the longest x1 235 us: local(): lax.psum((grad_qkv, grad_qv_bias, grad_out_weight, grad_out_bias, grad_ga...]
    pallas_call x0 -> x1, Pallas kernels: none -> 176 us  [run_layer(): pl.pallas_call(kernel, name='layer', out_shape=[jax.ShapeDtypeStruct(shap...]
    dot_general x36 -> x0, matrix products: 81.8 us -> none  [the longest x1 13.1 us: local(): jnp.dot(first_low, ffn_in, preferred_element_type=f32)]
    reduce_sum x20 -> x0, other arithmetic: 39.5 us -> none  [the longest x5 16.3 us: layer_norm(): return centre * lax.rsqrt(spread + NORM_EPS) * gain_row + bias_row]
    psum x1 -> x0, blocking collectives: 38.4 us -> none  [local(): lax.psum((grad_qkv, grad_qv_bias, grad_out_weight, grad_out_bias, grad_ga...]
    unnamed x2 -> x0, blocking collectives: 35.5 us -> none
    all_gather x1 -> x0, blocking collectives: 32.8 us -> none  [local(): lax.all_gather(passage_local, 'dp', axis=0, tiled=True)]
    unnamed x171 -> x13, local copies, waits for them, and re-layouts: 35.7 us -> 3.77 us
  transfers between devices with their start and end apart: 7 -> 0, of which waited for: 5 -> 0; matrix products, arithmetic and copies ran while one was open for 5% -> 0% of each run, Pallas kernels for 0% -> 0%
where the time goes in v1:
time: 197 us
  Pallas kernels  176 us (89%)
  local copies, waits for them, and re-layouts  10.1 us (5%)
  other arithmetic  8.05 us (4%)
  between operations  3.14 us (2%)
    pallas_call x1, Pallas kernels, run_layer(): pl.pallas_call(kernel, name='layer', out_shape=[jax.ShapeDtypeStruct(shap...  176 us

profile of v1, /device:TPU:0, one launch (start us, length us, event | category | flops | bytes accessed | tf_op | source)
XLA Modules:
  0.0 197.0 jit_solution(11264094302559171222)
XLA Ops:
  0.7 175.7 %layer.1 = (bf16[6,4,2,2,16,768]{5,4,3,2,1,0:T(8,128)(2,1)}, bf16[6,4,64,768]{3,2,1,0:T(8,128)(2,1)}, bf16[768,768]{1,0:T(8,128)(2,1)}, bf16[768,768]{1,0:T(8,12...) custom-call(bf16[1536,768]{1,0:T(8,128)(2,1)} %refs_0_.1, s32[1536]{0:T(1024)} %refs_1_.1, s32[3]{0:T(128)} %refs_2_.1, ...), custom_call_target="tpu_custom_call" | custom-call | tf_op jit(solution)/shard_map/layer/pallas_call | solution.py:901
  176.4 1.3 fusion.1
  179.0 1.7 slice_reduce_fusion
  180.6 0.0 copy-start.4
  180.7 2.0 fusion
  182.7 0.6 copy.40
  183.3 0.6 copy.41
  183.9 1.3 slice.57
  185.2 0.0 copy-done.4
  185.2 0.1 slice.56
  185.3 0.0 copy-start.1
  185.3 1.4 convert_bitcast_fusion
  186.6 0.9 slice_convert_fusion
  187.5 0.1 copy-done.1
  187.6 0.0 copy-start.3
  187.6 2.7 %bitcast_convert_fusion = f32[1536,768]{1,0:T(8,128)} fusion(bf16[6,4,64,768]{3,2,1,0:T(8,128)(2,1)S(1)} %copy-done.1), kind=kLoop, calls=%fused_computation | loop fusion | flops 1179648 | bytes 7077888 | tf_op jit(solution)/shard_map/convert_element_type | solution.py:938
  190.3 0.0 copy-done.3
  190.3 0.0 copy-start.2
  190.3 1.6 convert_element_type.30
  191.8 0.1 copy-done.2
  191.9 0.0 copy-start
  191.9 1.6 convert_element_type.31
  193.5 0.9 copy-done
  194.5 1.4 copy.43
  (2 shorter events, 0.1 us)
Async XLA Ops:
  180.6 4.5 %copy-start.4 = (bf16[768,768]{1,0:T(8,128)(2,1)S(1)}, bf16[768,768]{1,0:T(8,128)(2,1)}, u32[]{:S(2)}) copy-start(bf16[768,768]{1,0:T(8,128)(2,1)} %get-tuple-element.26) | copy-start | bytes 3538948
  185.3 2.3 %copy-start.1 = (bf16[6,4,64,768]{3,2,1,0:T(8,128)(2,1)S(1)}, bf16[6,4,64,768]{3,2,1,0:T(8,128)(2,1)}, u32[]{:S(2)}) copy-start(bf16[6,4,64,768]{3,2,1,0:T(8,128)(2,1)} %get-tuple-element.25) | copy-start | bytes 7077892
  187.6 2.7 %copy-start.3 = (bf16[768,768]{1,0:T(8,128)(2,1)S(1)}, bf16[768,768]{1,0:T(8,128)(2,1)}, u32[]{:S(2)}) copy-start(bf16[768,768]{1,0:T(8,128)(2,1)} %get-tuple-element.27) | copy-start | bytes 3538948
  190.3 1.7 copy-start.2
  191.9 2.5 %copy-start = (bf16[6,4,2,2,16,768]{5,4,3,2,1,0:T(8,128)(2,1)S(1)}, bf16[6,4,2,2,16,768]{5,4,3,2,1,0:T(8,128)(2,1)}, u32[]{:S(2)}) copy-start(bf16[6,4,2,2,16,768]{5,4,3,2,1,0:T(8,128)(2,1)} %get-tuple-element.23) | copy-start | bytes 7077892

commit v2 on v1

--- a/solution.py
+++ b/solution.py
@@ -133,38 +133,36 @@
 
     def w_send(k, at, d, idx):
         ref = wfs[k].at[t2, at]
-        cp(ref, ref, S_WRING, R.wr_r.at[idx], ring_to[d]).start()
+        cp(ref, ref, S_WRING, R.wr_r.at[k, idx], ring_to[d]).start()
 
     def w_on(k, at):
         ref = wfs[k].at[t2, at]
-        cp(ref, ref, S_WON, R.wf_r.at[0], core).start()
-
-    def w_start():
-        for k in range(2):
-            at = pl.ds(pl.multiple_of(r * share, share), share)
-            arrived(wfs[k].at[t2, at], R.wy_r.at[k])
-            for d in range(2):
-                w_send(k, unit(r, d), d, 0)
-                w_send(k, unit(r, 1 - d), d, 4)
+        cp(ref, ref, S_WON, R.wf_r.at[k], core).start()
+
+    def w_start(k):
+        at = pl.ds(pl.multiple_of(r * share, share), share)
+        arrived(wfs[k].at[t2, at], R.wy_r.at[k])
+        for d in range(2):
+            w_send(k, unit(r, d), d, 0)
+            w_send(k, unit(r, 1 - d), d, 4)
+        w_on(k, at)
+
+    def w_pass(k, s, lead):
+        idx = s - 1 if lead else s + 3
+        arrived(rb.at[0, :, 0], R.wr_r.at[k, idx])
+        for d in range(2):
+            at = unit(from_here(d, s), d if lead else 1 - d)
+            if s < (4 if lead else 3):
+                w_send(k, at, d, idx + 1)
             w_on(k, at)
 
-    def w_lead(s):
-        arrived(rb.at[0:2, :, 0], R.wr_r.at[s - 1])
-        for k in range(2):
-            for d in range(2):
-                at = unit(from_here(d, s), d)
-                if s < 4:
-                    w_send(k, at, d, s)
-                w_on(k, at)
-
-    def w_trail(s):
-        arrived(rb.at[0:2, :, 0], R.wr_r.at[3 + s])
-        for k in range(2):
-            for d in range(2):
-                at = unit(from_here(d, s), 1 - d)
-                if s < 3:
-                    w_send(k, at, d, 4 + s)
-                w_on(k, at)
+    def w_jobs(k):
+        return [lambda: w_start(k)] + [
+            lambda s=s, lead=lead: w_pass(k, s, lead)
+            for s, lead in ((1, True), (1, False), (2, True), (2, False), (3, True), (3, False), (4, True))
+        ]
+
+    wa, wb = w_jobs(0), w_jobs(1)
 
     for k in range(2):
         w_share(k).start()
@@ -289,12 +287,18 @@
             h1[part_at(b, i)] = out[:, b].reshape(32, width)
             R.x1_own[part_at(b, i)] = low4[:, b].reshape(32, width)
         x1[i, t] = low
-        ag0(x1.at[i, t], S_X1, R.gy_r.at[i], R.gc_r.at[i])
 
     def at_step(s, jobs):
         for i, job in jobs.items():
             pl.when(s == i)(job)
 
+    def both(*jobs):
+        def run():
+            for job in jobs:
+                job()
+
+        return run
+
     def fwd_step(s):
         attend(s)
         rs0(0, s)
@@ -303,22 +307,24 @@
         def _():
             rs1(s - 1)
 
-        at_step(s, {3: w_start})
-
-        @pl.when(s >= 3)
-        def _():
-            first_norm(s - 3)
+        at_step(s, {1: wa[0], 4: both(wa[1], wb[0]), 5: wa[2]})
 
     for one in loads[:3]:
         one.wait()
     loop(blocks, fwd_step)
     rs1(blocks - 1)
-    w_lead(1)
-    first_norm(blocks - 3)
-    w_trail(1)
-    first_norm(blocks - 2)
-    first_norm(blocks - 1)
-    w_lead(2)
+
+    wa[3]()
+
+    def norm_step(s):
+        first_norm(s)
+        at_step(s, {0: wb[1], 1: wa[4], 2: both(wb[2], wa[5]), 3: wb[3], 4: both(wa[6], wb[4]), 5: wa[7]})
+
+    loop(blocks, norm_step)
+    def x1_out(i):
+        ag0(x1.at[i, t], S_X1, R.gy_r.at[i], R.gc_r.at[i])
+
+    loop(blocks - 2, x1_out)
 
     for one in loads[3:]:
         one.wait()
@@ -332,43 +338,46 @@
         return (u * cdf).astype(bf16), (cdf + u * pdf).astype(bf16)
 
     wide = R.wide
-    wide[...] = jnp.zeros((own, width), f32)
-
-    def own_fwd(j):
-        q = jnp.where(j == 0, t, jnp.where(j == 1, t1, jnp.where(j == 2, t2, t3)))
+    act_own = R.da
+
+    def nth(j):
+        return jnp.where(j == 0, t, jnp.where(j == 1, t1, jnp.where(j == 2, t2, t3)))
+
+    def own_in(j):
+        q = nth(j)
         u = dot(R.x1_own[...], wfs[0][q]) + R.bias1[q, 0:1]
         a, sl = gelu(u)
         R.slope_own[q] = sl
-        wide[...] += dot(a, wfs[1][q])
+        act_own[:, q] = a.reshape(blocks, 2, 2, 16, width)
+
+    def own_out(j):
+        q = nth(j)
+        wide[...] += dot(act_own[:, q].reshape(own, width), wfs[1][q])
+
+    def x1_on(i):
+        ag1(x1.at[i, t2], S_X1, R.gy_r.at[i], R.gc_r.at[i])
 
     def quarter_fwd(i):
-        ag1(x1.at[i, t2], S_X1, R.gy_r.at[i], R.gc_r.at[i])
         arrived(x1.at[i, 0:2], R.gc_r.at[i])
         u = dot(x1[i].reshape(BLK, width), wfs[0][t]) + R.bias1[t, 0:1]
         a, sl = gelu(u)
         act[i] = a.reshape(4, 2, 2, 16, width)
         slope[i] = sl.reshape(4, 2, 2, 16, width)
 
-    def middle(s):
-        @pl.when(s < 2)
-        def _():
-            own_fwd(s)
-
-        @pl.when((s >= 2) & (s < blocks + 2))
-        def _():
-            quarter_fwd(s - 2)
-
-        at_step(s, {0: lambda: w_trail(2), 1: lambda: w_lead(3), 3: lambda: w_trail(3), 5: lambda: w_lead(4)})
-
-        @pl.when(s >= blocks + 2)
-        def _():
-            @pl.when(s == blocks + 3)
-            def _():
-                arrived(R.wf1.at[0:2], R.wf_r.at[0])
-
-            own_fwd(s - blocks)
-
-    loop(blocks + 4, middle)
+    def own_step(s):
+        own_in(s)
+        at_step(
+            s, {0: wb[5], 1: both(wb[6], lambda: arrived(R.wf1.at[0], R.wf_r.at[0])), 2: wb[7]}
+        )
+
+    loop(4, own_step)
+    wide[...] = jnp.zeros((own, width), f32)
+
+    def out_step(s):
+        at_step(s, {3: lambda: arrived(R.wf2.at[0], R.wf_r.at[1])})
+        own_out(s)
+
+    loop(4, out_step)
 
     low_out = R.low
 
@@ -460,8 +469,6 @@
     du_all = slope
 
     def quarter_bwd(b):
-        arrived(df.at[:, 0:2, :, b], R.fc_r.at[b])
-
         def one(j):
             at = pl.ds(2 * j, 2)
             dg = dot_t(df[at, :, :, b].reshape(BLK, width), wfs[1][t])
@@ -472,6 +479,7 @@
         loop(blocks // 2, one)
 
     second_back(1)
+    loop(blocks, x1_out, blocks - 2)
 
     arrived(firsts.at[0:3], R.fi_r.at[0])
     hw = width // 2
@@ -505,6 +513,7 @@
                 target_at = jnp.where(row_q == 8 * tt + 2 * b + k, at, target_at)
 
     own_bwd(1)
+    loop(blocks - 2, x1_on)
 
     arrived(mail.at[1:], R.dp_r.at[0])
     pe = R.pe
@@ -541,7 +550,10 @@
     back[dp] = dpe[dp]
 
     df_on(1)
-    da_on(1)
+    loop(blocks - 2, quarter_fwd)
+    loop(blocks, x1_on, blocks - 2)
+    loop(blocks, quarter_fwd, blocks - 2)
+    arrived(df.at[:, 0:2, :, 1], R.fc_r.at[1])
     quarter_bwd(1)
 
     @pl.when(c == 0)
@@ -564,19 +576,11 @@
     second_back(0)
     own_bwd(0)
 
-    out = R.layer_out
-    out_own = pltpu.make_async_copy(low_out, out.at[:, t], R.ss.at[S_OUTL])
-    out_own.start()
-    cp(low_out, out.at[:, t], S_OUT, R.lo_r.at[0], ypeer).start()
-    cp(low_out, out.at[:, t], S_OUT, R.lo_r.at[1], core).start()
-
     sums[6:7] = jnp.where(t == 0, loss, 0.0) + jnp.zeros((1, width), f32)
     tsum = R.tsum
     tsum[t] = sums[0:8]
     for mate in mates:
         cp(tsum.at[t], tsum.at[t], S_TSUM, R.ts_r.at[0], mate).start()
-    df_on(0)
-    quarter_bwd(0)
 
     grads = (R.ga1, R.ga2, R.ga3)
     outs = (R.o1, R.o2, R.o3)
@@ -653,22 +657,40 @@
             lambda: gather_on(k, 4, True),
         ]
 
-    tile = BLK
-
-    def grad2(j):
-        at = pl.ds(pl.multiple_of(j * tile, tile), tile)
-        grads[1][at] = dot_l(act[..., at].reshape(rows, tile), df[...].reshape(rows, width)).astype(bf16)
-
-    loop(quarter // tile, grad2)
+    da_on(1)
+    part_all = rows // 2
+
+    def grad2(b):
+        def one(j):
+            at = pl.ds(pl.multiple_of(j * BLK, BLK), BLK)
+            new = dot_l(act[:, :, :, b, :, at].reshape(part_all, BLK), df[:, :, :, b].reshape(part_all, width))
+            if b == 0:
+                new = new + grads[1][at].astype(f32)
+            grads[1][at] = new.astype(bf16)
+
+        loop(quarter // BLK, one)
+
+    def grad1(b):
+        def one(j):
+            at = pl.ds(pl.multiple_of(j * BLK, BLK), BLK)
+            x1_part = x1[...].reshape(blocks, 4, 2, 2, 16, width)[:, :, :, b].reshape(part_all, width)
+            new = dot_l(x1_part, du_all[:, :, :, b, :, at].reshape(part_all, BLK))
+            if b == 0:
+                new = new + grads[0][:, at].astype(f32)
+            grads[0][:, at] = new.astype(bf16)
+
+        loop(quarter // BLK, one)
+
+    grad2(1)
+    grad1(1)
+    df_on(0)
+    arrived(df.at[:, 0:2, :, 0], R.fc_r.at[0])
+    grad2(0)
     ring_start(1)
+    quarter_bwd(0)
+    grad1(0)
+    ring_start(0)
     da_on(0)
-
-    def grad1(j):
-        at = pl.ds(pl.multiple_of(j * tile, tile), tile)
-        grads[0][:, at] = dot_l(x1[...].reshape(rows, width), du_all[..., at].reshape(rows, tile)).astype(bf16)
-
-    loop(quarter // tile, grad1)
-    ring_start(0)
 
     dq_all, dk_all, dv_all = R.q, R.k, R.v
 
@@ -744,6 +766,12 @@
 
     loop(blocks, back_step)
 
+    out = R.layer_out
+    out_own = pltpu.make_async_copy(low_out, out.at[:, t], R.ss.at[S_OUTL])
+    out_own.start()
+    cp(low_out, out.at[:, t], S_OUT, R.lo_r.at[0], ypeer).start()
+    cp(low_out, out.at[:, t], S_OUT, R.lo_r.at[1], core).start()
+
     grads[2][0:local_width] = dot_l(dq_all[...], hid[...]).astype(bf16)
     grads[2][local_width : 2 * local_width] = dot_l(dk_all[...], hid[...]).astype(bf16)
     grads[2][2 * local_width : 3 * local_width] = dot_l(dv_all[...], hid[...]).astype(bf16)
@@ -773,6 +801,7 @@
 
     loop(n_dp, vec_add, 1)
     R.vec_out[...] = sums[...]
+    R.firsts_out[...] = firsts[...]
     piece = x1.at[:, 0]
     arrived(piece, R.lo_r.at[0])
     cp(out.at[:, t2], out.at[:, t2], S_OUT, R.lo_r.at[1], core).start()
@@ -830,6 +859,7 @@
         o2=(any_, (width, width), bf16),
         o3=(any_, (width, width), bf16),
         vec_out=(vmem, (16, width), f32),
+        firsts_out=(vmem, (4, 16, width), bf16),
     )
     scratch = dict(
         hid=vm((rows, width), bf16),
@@ -883,7 +913,7 @@
         rb=vm((3, 2, RING - 1, share, width), bf16),
         load_sem=dma((6,)),
         ss=dma((24,)),
-        wc_r=dma((1,)), wy_r=dma((2,)), wf_r=dma((1,)), wr_r=dma((7,)), bi_r=dma((1,)),
+        wc_r=dma((1,)), wy_r=dma((2,)), wf_r=dma((2,)), wr_r=dma((2, 7)), bi_r=dma((1,)),
         rc_r=dma((2, blocks)), ry_r=dma((2, blocks)),
         gy_r=dma((blocks,)), gc_r=dma((blocks,)),
         fy_r=dma((2,)), fc_r=dma((2,)), ay_r=dma((2,)), ac_r=dma((2,)),
@@ -909,6 +939,59 @@
             collective_id=0, has_side_effects=True, vmem_limit_bytes=64 * 2**20
         ),
     )(*[ins[n] for n in ins_at])
+
+
+def run_finish(lout, gin, o1, o2, o3, sums, firsts, slots, queries, local_width, n_dp):
+    rows, width = lout.shape
+    steps = rows // BLK
+    shapes = (
+        ((rows, width), bf16), ((queries, width), bf16), ((2 * slots, width), bf16), ((1, 1), f32),
+        ((rows, width), f32), ((3 * local_width, width), f32), ((2, local_width), f32), ((local_width, width), f32),
+        ((width,), f32), ((width,), f32), ((width,), f32), ((width, width), f32), ((width,), f32),
+        ((width, width), f32), ((width,), f32), ((width,), f32), ((width,), f32),
+    )
+    big = (0, 4, 5, 7, 11, 13)
+
+    def whole(shape):
+        return pl.BlockSpec(shape, lambda i: (0,) * len(shape))
+
+    def cut(count, offset=0):
+        return pl.BlockSpec((count // steps, width), lambda i: (i + offset, 0))
+
+    def kernel(lout, gin, o1, o2, o3a, o3b, sums, firsts, *outs):
+        outs[0][...] = lout[...]
+        outs[4][...] = gin[...].astype(f32)
+        outs[5][...] = o3a[...].astype(f32)
+        outs[7][...] = o3b[...].astype(f32)
+        outs[11][...] = o1[...].astype(f32)
+        outs[13][...] = o2[...].astype(f32)
+
+        @pl.when(pl.program_id(0) == 0)
+        def _():
+            tiles = [firsts[k].astype(f32) for k in range(4)]
+            query = [tiles[q % 8 // 2][2 * (q // 8) + q % 2 : 2 * (q // 8) + q % 2 + 1] for q in range(queries)]
+            outs[1][...] = jnp.concatenate(query, axis=0).astype(bf16)
+            passage = [tiles[2 * (p % 2)][6 + p // 2 : 7 + p // 2] for p in range(2 * slots)]
+            outs[2][...] = jnp.concatenate(passage, axis=0).astype(bf16)
+            outs[3][...] = (sums[6:7, 0:1] + sums[7:8, 0:1]) * (1.0 / (queries * n_dp))
+            outs[6][...] = sums[9:11, 0:local_width]
+            for at, row in ((8, 5), (9, 3), (10, 4), (12, 8), (14, 2), (15, 0), (16, 1)):
+                outs[at][...] = sums[row : row + 1].reshape(width)
+
+    specs = [whole(shape) for shape, _ in shapes]
+    for at in big:
+        specs[at] = cut(shapes[at][0][0])
+    return pl.pallas_call(
+        kernel,
+        name="finish",
+        grid=(steps,),
+        out_shape=[jax.ShapeDtypeStruct(shape, kind) for shape, kind in shapes],
+        in_specs=[
+            cut(rows), cut(rows), cut(width), cut(width), cut(3 * local_width),
+            cut(local_width, 3 * local_width // (local_width // steps)), whole((16, width)), whole((4, 16, width)),
+        ],
+        out_specs=specs,
+    )(lout, gin, o1, o2, o3, o3, sums, firsts)
 
 
 def local(
@@ -927,17 +1010,13 @@
         w2=ffn_out, fb=ffn_out_bias, g2=norm2_gain, n2b=norm2_bias,
         upstream=upstream.reshape(blocks, 4, 2, 2, 16, width),
     )
-    lout, gin, o1, o2, o3, sums = run_layer(n_dp, ins, (rows, width, slots, queries, local_width))
-    lout = lout.reshape(rows, width)
-    slot_rows = slots * SLOT_LEN
-    passage = lout[:slot_rows].reshape(2 * slots, SLOT_LEN // 2, width)[:, 0]
-    query = lout[slot_rows:].reshape(queries, QRY_LEN, width)[:, 0]
-    qkv = o3[: 3 * local_width].reshape(3, local_width, width)
-    loss = (sums[6, 0] + sums[7, 0]) / (queries * n_dp)
+    lout, gin, o1, o2, o3, sums, firsts = run_layer(n_dp, ins, (rows, width, slots, queries, local_width))
+    lout, gin = lout.reshape(rows, width), gin.reshape(rows, width)
+    outs = run_finish(lout, gin, o1, o2, o3, sums, firsts, slots, queries, local_width, n_dp)
+    lout, query, passage, loss, gin, qkv, qv, gout, gob, gg1, gn1b, gf1, gb1, gf2, gfb, gg2, gn2b = outs
+    qkv = qkv.reshape(3, local_width, width).transpose(0, 2, 1)
     return (
-        lout, query, passage, loss, gin.reshape(rows, width).astype(f32),
-        qkv.transpose(0, 2, 1).astype(f32), sums[9:11, :local_width], o3[3 * local_width :].astype(f32),
-        sums[5], sums[3], sums[4], o1.astype(f32), sums[8], o2.astype(f32), sums[2], sums[0], sums[1],
+        lout, query, passage, loss.reshape(()), gin, qkv, qv, gout, gob, gg1, gn1b, gf1, gb1, gf2, gfb, gg2, gn2b
     )
 
 

time: 197 us -> 167 us (0.85)
  local copies, waits for them, and re-layouts: 10.1 us -> 0 us
  Pallas kernels: 176 us -> 166 us
  other arithmetic: 8.05 us -> 0 us
  between operations: 3.14 us -> 0.83 us
    pallas_call x1, Pallas kernels: 176 us -> 157 us  [run_layer(): pl.pallas_call(kernel, name='layer', out_shape=[jax.ShapeDtypeStruct(shap...]
    pallas_call x0 -> x1, Pallas kernels: none -> 9.41 us  [run_finish(): pl.pallas_call(kernel, name='finish', grid=(steps,), out_shape=[jax.Shape...]
    convert_element_type x5 -> x0, other arithmetic: 8.05 us -> none  [the longest x1 2.7 us: local(): gin.reshape(rows, width).astype(f32)]
    slice x7 -> x0, local copies, waits for them, and re-layouts: 6.3 us -> none  [the longest x2 1.97 us: local(): passage = lout[:slot_rows].reshape(2 * slots, SLOT_LEN // 2, width)[:, 0]]
    unnamed x13 -> x0, local copies, waits for them, and re-layouts: 3.77 us -> none
where the time goes in v2:
time: 167 us
  Pallas kernels  166 us (99%)
    pallas_call x1, Pallas kernels, run_layer(): pl.pallas_call(kernel, name='layer', out_shape=[jax.ShapeDtypeStruct(shap...  157 us
    pallas_call x1, Pallas kernels, run_finish(): pl.pallas_call(kernel, name='finish', grid=(steps,), out_shape=[jax.Shape...  9.41 us

profile of v2, /device:TPU:0, one launch (start us, length us, event | category | flops | bytes accessed | tf_op | source)
XLA Modules:
  0.0 166.8 jit_solution(6636326840955555035)
XLA Ops:
  0.7 156.6 %layer.1 = (bf16[6,4,2,2,16,768]{5,4,3,2,1,0:T(8,128)(2,1)}, bf16[6,4,64,768]{3,2,1,0:T(8,128)(2,1)}, bf16[768,768]{1,0:T(8,128)(2,1)}, bf16[768,768]{1,0:T(8,12...) custom-call(bf16[1536,768]{1,0:T(8,128)(2,1)} %refs_0_.1, s32[1536]{0:T(1024)} %refs_1_.1, ...), custom_call_target="tpu_custom_call" | custom-call | tf_op jit(solution)/shard_map/layer/pallas_call | solution.py:931
  157.2 9.4 %finish.1 = (bf16[1536,768]{1,0:T(8,128)(2,1)}, bf16[24,768]{1,0:T(8,128)(2,1)}, bf16[6,768]{1,0:T(8,128)(2,1)}, f32[1,1]{1,0:T(1,128)}, f32[1536,768]{1,0:T(8,1...) custom-call(bf16[1536,768]{1,0:T(8,128)(2,1)} %bitcast.9, ...), custom_call_target="tpu_custom_call" | custom-call | tf_op jit(solution)/shard_map/finish/pallas_call | solution.py:984

commit v3 on v2

--- a/solution.py
+++ b/solution.py
@@ -52,7 +52,6 @@
     loss_scale = 2.0 / math.sqrt(width)
     quarter = width
     own = blocks * PIECE
-    part_rows = own // 2
 
     dp = lax.axis_index("dp")
     t = lax.axis_index("tensor")
@@ -81,7 +80,7 @@
         return lax.rem(dp + k, n_dp)
 
     (S_SHARE, S_WCORE, S_WRING, S_WON, S_BIAS, S_CORE0, S_Y0, S_CORE1, S_Y1, S_X1, S_FIRST, S_DF, S_DA, S_OUT, S_MAIL,
-     S_BACK, S_VEC, S_TSUM, S_RING, S_GATHER, S_LOCAL, S_GLOCAL, S_GCORE, S_OUTL) = range(24)
+     S_BACK, S_VEC, S_TSUM, S_RING, S_GATHER, S_LOCAL, S_GLOCAL, S_GCORE, S_OUTL, S_PART) = range(25)
 
     def cp(src, dst, kind, rsem, dev):
         return pltpu.make_async_remote_copy(
@@ -263,6 +262,17 @@
     vec = SimpleNamespace(
         ob=vec_of(R.ob), g1=vec_of(R.g1), n1b=vec_of(R.n1b), fb=vec_of(R.fb), g2=vec_of(R.g2), n2b=vec_of(R.n2b)
     )
+    first_at = [(slots + b) * PIECE + 32 * k for b in range(blocks - slots) for k in range(2)]
+    first_at += [s * PIECE for s in range(slots)]
+
+    def pick(ref):
+        rows_of = [ref[at : at + 1] for at in first_at]
+        return jnp.concatenate(rows_of + [jnp.zeros((16 - len(first_at), ref.shape[1]), f32)], axis=0)
+
+    def pick_low(ref):
+        rows_of = [ref[at : at + 16].astype(f32)[0:1] for at in first_at]
+        return jnp.concatenate(rows_of + [jnp.zeros((16 - len(first_at), ref.shape[1]), f32)], axis=0)
+
     x1 = R.x1
     h1, n1, n2 = R.h1, R.n1, R.n2
     rstd1, rstd2 = R.rstd1, R.rstd2
@@ -270,23 +280,16 @@
     def own_rows(i):
         return pl.ds(pl.multiple_of(i * BLK + t * PIECE, PIECE), PIECE)
 
-    def part_at(b, i):
-        return pl.ds(pl.multiple_of(b * part_rows + i * 32, 32), 32)
+    def piece_at(i):
+        return pl.ds(pl.multiple_of(i * PIECE, PIECE), PIECE)
 
     def first_norm(i):
         v = hid[own_rows(i)].astype(f32) + rs2(i) + vec.ob
         n, rstd, out = norm_fwd(v, vec.g1, vec.n1b)
-        wide_rstd = jnp.broadcast_to(rstd, (PIECE, 128)).reshape(2, 2, 16, 128)
-        n = n.reshape(2, 2, 16, width)
-        low = out.astype(bf16)
-        out = out.reshape(2, 2, 16, width)
-        low4 = low.reshape(2, 2, 16, width)
-        for b in range(2):
-            n1[part_at(b, i)] = n[:, b].reshape(32, width)
-            rstd1[part_at(b, i)] = wide_rstd[:, b].reshape(32, 128)
-            h1[part_at(b, i)] = out[:, b].reshape(32, width)
-            R.x1_own[part_at(b, i)] = low4[:, b].reshape(32, width)
-        x1[i, t] = low
+        n1[piece_at(i)] = n
+        rstd1[piece_at(i)] = jnp.broadcast_to(rstd, (PIECE, 128))
+        h1[piece_at(i)] = out
+        x1[i, t] = out.astype(bf16)
 
     def at_step(s, jobs):
         for i, job in jobs.items():
@@ -324,6 +327,14 @@
     def x1_out(i):
         ag0(x1.at[i, t], S_X1, R.gy_r.at[i], R.gc_r.at[i])
 
+    x1f = R.x1f
+    x1f[t] = pick(h1).astype(bf16)
+
+    def tile_out(tiles, which):
+        for mate in mates:
+            cp(tiles.at[t], tiles.at[t], S_FIRST, R.fi_r.at[which], mate).start()
+
+    tile_out(x1f, 1)
     loop(blocks - 2, x1_out)
 
     for one in loads[3:]:
@@ -345,10 +356,10 @@
 
     def own_in(j):
         q = nth(j)
-        u = dot(R.x1_own[...], wfs[0][q]) + R.bias1[q, 0:1]
+        u = dot(x1[:, t].reshape(own, width), wfs[0][q]) + R.bias1[q, 0:1]
         a, sl = gelu(u)
         R.slope_own[q] = sl
-        act_own[:, q] = a.reshape(blocks, 2, 2, 16, width)
+        act_own[:, q] = a.reshape(blocks, PIECE, width)
 
     def own_out(j):
         q = nth(j)
@@ -361,8 +372,8 @@
         arrived(x1.at[i, 0:2], R.gc_r.at[i])
         u = dot(x1[i].reshape(BLK, width), wfs[0][t]) + R.bias1[t, 0:1]
         a, sl = gelu(u)
-        act[i] = a.reshape(4, 2, 2, 16, width)
-        slope[i] = sl.reshape(4, 2, 2, 16, width)
+        act[blk(i)] = a
+        slope[blk(i)] = sl
 
     def own_step(s):
         own_in(s)
@@ -387,99 +398,94 @@
         n2[at] = n
         rstd2[at] = jnp.broadcast_to(rstd, (PIECE, 128))
         h1[at] = out
-        b = lax.div(j, blocks // 2)
-        i = 2 * lax.rem(j, blocks // 2)
-        low_out[pl.ds(i, 2), :, b] = out.astype(bf16).reshape(2, 2, 16, width)
+        low_out[j] = out.astype(bf16)
 
     loop(blocks, second_norm)
 
     firsts = R.firsts
     stage = R.stage
     stage[...] = jnp.zeros((16, width), f32)
-    for b in range(blocks - slots):
-        for k in range(2):
-            at = (slots + b) * 32 + 16 * k
-            stage[2 * b + k : 2 * b + k + 1] = h1[at : at + 1]
-    for s in range(slots):
-        stage[6 + s : 7 + s] = h1[32 * s : 32 * s + 1]
-    firsts[t] = stage[...].astype(bf16)
-    for mate in mates:
-        cp(firsts.at[t], firsts.at[t], S_FIRST, R.fi_r.at[0], mate).start()
+    firsts[t] = pick(h1).astype(bf16)
+    tile_out(firsts, 0)
+    loop(blocks, x1_out, blocks - 2)
 
     sums = R.sums
     sums[...] = jnp.zeros((16, width), f32)
-    adds = R.adds
     up, dv2, df, da = R.up, R.n2, R.df, R.da
     dv1 = R.h1
+    dfl, dal = R.dfl, R.dal
+    near = blocks // 2
 
     def colsum(v):
         return jnp.sum(v, axis=0, keepdims=True)
 
-    def second_back(b):
-        def one(i):
-            at = part_at(b, i)
-            dy = up[i, :, b].reshape(32, width).astype(f32)
-            if b == 0:
-                row = lax.broadcasted_iota(jnp.int32, (32, 1), 0)
-                dy = dy + jnp.where(row == 0, adds[i, 0:1], 0.0) + jnp.where(row == 16, adds[i, 1:2], 0.0)
-            n = n2[at]
-            sums[0:1] += colsum(dy * n)
-            sums[1:2] += colsum(dy)
-            dv = norm_bwd(dy, n, rstd2[at][:, 0:1], vec.g2)
-            dv2[at] = dv
-            low = dv.astype(bf16)
-            sums[2:3] += colsum(low.astype(f32))
-            df[i, t, :, b] = low.reshape(2, 16, width)
-
-        loop(blocks, one)
-        ag0(df.at[:, t, :, b], S_DF, R.fy_r.at[b], R.fc_r.at[b])
-
-    def own_bwd(b):
-        at = pl.ds(b * part_rows, part_rows)
-        wide[at] = dv2[at]
-
-        def one(q):
-            dg = dot_t(df[:, t, :, b].reshape(part_rows, width), wfs[1][q])
-            du = (dg * R.slope_own[q, at].astype(f32)).astype(bf16)
-            wide[at] += dot_t(du, wfs[0][q])
-
-        loop(4, one)
-
-        def first_back(i):
-            at = part_at(b, i)
-            dy = wide[at]
-            n = n1[at]
-            sums[3:4] += colsum(dy * n)
-            sums[4:5] += colsum(dy)
-            dv = norm_bwd(dy, n, rstd1[at][:, 0:1], vec.g1)
-            dv1[at] = dv
-            low = dv.astype(bf16)
-            sums[5:6] += colsum(low.astype(f32))
-            da[i, t, :, b] = low.reshape(2, 16, width)
-
-        loop(blocks, first_back)
-        ag0(da.at[:, t, :, b], S_DA, R.ay_r.at[b], R.ac_r.at[b])
-
-    def df_on(b):
-        ag1(df.at[:, t2, :, b], S_DF, R.fy_r.at[b], R.fc_r.at[b])
-
-    def da_on(b):
-        ag1(da.at[:, t2, :, b], S_DA, R.ay_r.at[b], R.ac_r.at[b])
+    tile_n1, tile_n2 = pick(n1), pick(n2)
+    tile_r1, tile_r2 = pick(rstd1)[:, 0:1], pick(rstd2)[:, 0:1]
+    tile_up = pick_low(up.reshape(own, width))
+
+    def norm2_back(dy, n, rstd):
+        sums[0:1] += colsum(dy * n)
+        sums[1:2] += colsum(dy)
+        dv = norm_bwd(dy, n, rstd, vec.g2)
+        low = dv.astype(bf16)
+        sums[2:3] += colsum(low.astype(f32))
+        return dv, low
+
+    def norm1_back(dy, n, rstd):
+        sums[3:4] += colsum(dy * n)
+        sums[4:5] += colsum(dy)
+        dv = norm_bwd(dy, n, rstd, vec.g1)
+        low = dv.astype(bf16)
+        sums[5:6] += colsum(low.astype(f32))
+        return dv, low
+
+    def second_back(i):
+        at = piece_at(i)
+        row = lax.broadcasted_iota(jnp.int32, (PIECE, 1), 0)
+        is_query = jnp.where(i >= slots, 1, 0)
+        late = jnp.where(row == 0, jnp.maximum(is_query, 1 - c), jnp.where(row == 32, is_query, 0))
+        dy = jnp.where(late == 0, up[i].astype(f32), 0.0)
+        dv, low = norm2_back(dy, n2[at], rstd2[at][:, 0:1])
+        dv2[at] = dv
+        df[i, t] = low
+
+    def halves(p):
+        return pl.ds(p * near, near)
+
+    for p in range(2):
+        loop((p + 1) * near, second_back, p * near)
+        ag0(df.at[halves(p), t], S_DF, R.fy_r.at[p], R.fc_r.at[p])
+    wide[...] = dv2[...]
+
+    def own_bwd(q):
+        dg = dot_t(df[:, t].reshape(own, width), wfs[1][q])
+        du = (dg * R.slope_own[q].astype(f32)).astype(bf16)
+        wide[...] += dot_t(du, wfs[0][q])
+
+    def first_back(i):
+        at = piece_at(i)
+        dv, low = norm1_back(wide[at], n1[at], rstd1[at][:, 0:1])
+        dv1[at] = dv
+        da[i, t] = low
+
+    def df_on(p):
+        ag1(df.at[halves(p), t2], S_DF, R.fy_r.at[p], R.fc_r.at[p])
+
+    def da_on(p):
+        ag1(da.at[halves(p), t2], S_DA, R.ay_r.at[p], R.ac_r.at[p])
+
+    def here(full, p, sem):
+        arrived(full.at[halves(p), 0:2], sem.at[p])
 
     du_all = slope
 
-    def quarter_bwd(b):
-        def one(j):
-            at = pl.ds(2 * j, 2)
-            dg = dot_t(df[at, :, :, b].reshape(BLK, width), wfs[1][t])
-            du = (dg * slope[at, :, :, b].reshape(BLK, width).astype(f32)).astype(bf16)
-            sums[8:9] += colsum(du.astype(f32))
-            du_all[at, :, :, b] = du.reshape(2, 4, 2, 16, width)
-
-        loop(blocks // 2, one)
-
-    second_back(1)
-    loop(blocks, x1_out, blocks - 2)
+    def quarter_bwd(i):
+        dg = dot_t(df[i].reshape(BLK, width), wfs[1][t])
+        du = (dg * slope[blk(i)].astype(f32)).astype(bf16)
+        sums[8:9] += colsum(du.astype(f32))
+        du_all[blk(i)] = du
+
+    loop(2, own_bwd)
 
     arrived(firsts.at[0:3], R.fi_r.at[0])
     hw = width // 2
@@ -512,8 +518,11 @@
                 at = lax.div(slot, slots) * 8 + lax.rem(pos, 2) * 3 + lax.rem(slot, slots)
                 target_at = jnp.where(row_q == 8 * tt + 2 * b + k, at, target_at)
 
-    own_bwd(1)
-    loop(blocks - 2, x1_on)
+    loop(4, own_bwd, 2)
+    loop(blocks, first_back)
+
+    def da_out(p):
+        ag0(da.at[halves(p), t], S_DA, R.ay_r.at[p], R.ac_r.at[p])
 
     arrived(mail.at[1:], R.dp_r.at[0])
     pe = R.pe
@@ -549,12 +558,14 @@
 
     back[dp] = dpe[dp]
 
-    df_on(1)
+    loop(blocks, x1_on)
     loop(blocks - 2, quarter_fwd)
-    loop(blocks, x1_on, blocks - 2)
+    df_on(0)
     loop(blocks, quarter_fwd, blocks - 2)
-    arrived(df.at[:, 0:2, :, 1], R.fc_r.at[1])
-    quarter_bwd(1)
+    arrived(x1f.at[0:3], R.fi_r.at[1])
+    x1_late = x1f[...].reshape(64, width)
+    act_late, slope_late = gelu(dot(x1_late, wfs[0][t]) + R.bias1[t, 0:1])
+    R.act_late[...] = act_late
 
     @pl.when(c == 0)
     def _():
@@ -567,20 +578,15 @@
         loop(n_dp, add, 1)
 
     mine_q = dqe[pl.ds(pl.multiple_of(t * 8, 8), 8)]
-    is_c0 = jnp.where(c == 0, 1.0, 0.0).astype(f32)
-    adds[...] = jnp.zeros(adds.shape, f32)
+    row_l = lax.broadcasted_iota(jnp.int32, (16, 1), 0)
     for s in range(slots):
-        adds[s, 0:1] = jnp.where(y == 0, stage[s : s + 1], stage[3 + s : 4 + s]) * is_c0
-    for b in range(blocks - slots):
-        adds[slots + b, 0:2] = mine_q[2 * b : 2 * b + 2]
-    second_back(0)
-    own_bwd(0)
-
-    sums[6:7] = jnp.where(t == 0, loss, 0.0) + jnp.zeros((1, width), f32)
-    tsum = R.tsum
-    tsum[t] = sums[0:8]
-    for mate in mates:
-        cp(tsum.at[t], tsum.at[t], S_TSUM, R.ts_r.at[0], mate).start()
+        stage[8 + s : 9 + s] = jnp.where(y == 0, stage[s : s + 1], stage[3 + s : 4 + s])
+    grad_late = jnp.concatenate([mine_q[0:6], stage[8 : 8 + slots], jnp.zeros((16 - 6 - slots, width), f32)], axis=0)
+    is_late = (row_l < 6) | ((row_l < 6 + slots) & (c == 0))
+    dv2_late, low = norm2_back(jnp.where(is_late, tile_up + grad_late, 0.0), tile_n2, tile_r2)
+    dfl[t] = low
+    tile_out(dfl, 2)
+    da_out(0)
 
     grads = (R.ga1, R.ga2, R.ga3)
     outs = (R.o1, R.o2, R.o3)
@@ -657,45 +663,82 @@
             lambda: gather_on(k, 4, True),
         ]
 
-    da_on(1)
-    part_all = rows // 2
-
-    def grad2(b):
+    half_rows = rows // 2
+
+    def flat(full, p):
+        return full[halves(p)].reshape(half_rows, width)
+
+    def rows_of(p):
+        return pl.ds(p * half_rows, half_rows)
+
+    def grad2(p):
         def one(j):
             at = pl.ds(pl.multiple_of(j * BLK, BLK), BLK)
-            new = dot_l(act[:, :, :, b, :, at].reshape(part_all, BLK), df[:, :, :, b].reshape(part_all, width))
-            if b == 0:
-                new = new + grads[1][at].astype(f32)
+            new = dot_l(act[rows_of(p), at], flat(df, p))
+            if p == 1:
+                new = new + grads[1][at].astype(f32) + dot_l(R.act_late[:, at], dfl[...].reshape(64, width))
             grads[1][at] = new.astype(bf16)
 
         loop(quarter // BLK, one)
 
-    def grad1(b):
+    def grad1(p):
         def one(j):
             at = pl.ds(pl.multiple_of(j * BLK, BLK), BLK)
-            x1_part = x1[...].reshape(blocks, 4, 2, 2, 16, width)[:, :, :, b].reshape(part_all, width)
-            new = dot_l(x1_part, du_all[:, :, :, b, :, at].reshape(part_all, BLK))
-            if b == 0:
-                new = new + grads[0][:, at].astype(f32)
+            new = dot_l(flat(x1, p), du_all[rows_of(p), at])
+            if p == 1:
+                new = new + grads[0][:, at].astype(f32) + dot_l(x1f[...].reshape(64, width), R.du_late[:, at])
             grads[0][:, at] = new.astype(bf16)
 
         loop(quarter // BLK, one)
 
+    here(df, 0, R.fc_r)
+    grad2(0)
+    df_on(1)
+    loop(near, quarter_bwd)
+    arrived(dfl.at[0:3], R.fi_r.at[2])
+    here(df, 1, R.fc_r)
     grad2(1)
+    ring_start(1)
+
+    dg_late = dot_t(dfl[...].reshape(64, width), wfs[1][t])
+    du_late = (dg_late * slope_late.astype(f32)).astype(bf16)
+    sums[8:9] += colsum(du_late.astype(f32))
+    R.du_late[...] = du_late
+    parts = R.parts
+    parts[...] = dot_t(du_late, wfs[0][t]).astype(bf16).reshape(4, 16, width)
+    for tt, mate in zip((t1, t2, t3), mates):
+        cp(parts.at[tt], R.parts_in.at[t], S_PART, R.fi_r.at[4], mate).start()
+    loop(blocks, quarter_bwd, near)
+    jobs1, jobs0, jobs2 = ring_jobs(1), ring_jobs(0), ring_jobs(2)
+    grad1(0)
+    jobs1[0]()
+    da_on(0)
+    arrived(dfl.at[0:3], R.fi_r.at[4])
+    late_sum = dv2_late + parts[t].astype(f32)
+    for tt in (t1, t2, t3):
+        late_sum = late_sum + R.parts_in[tt].astype(f32)
+    dv1_late, low = norm1_back(jnp.where(is_late, late_sum, 0.0), tile_n1, tile_r1)
+    for j, at in enumerate(first_at):
+        dv1[at : at + 1] += dv1_late[j : j + 1]
+    dal[t] = low
+    tile_out(dal, 3)
+    da_out(1)
+    sums[6:7] = jnp.where(t == 0, loss, 0.0) + jnp.zeros((1, width), f32)
+    tsum = R.tsum
+    tsum[t] = sums[0:8]
+    for mate in mates:
+        cp(tsum.at[t], tsum.at[t], S_TSUM, R.ts_r.at[0], mate).start()
     grad1(1)
-    df_on(0)
-    arrived(df.at[:, 0:2, :, 0], R.fc_r.at[0])
-    grad2(0)
-    ring_start(1)
-    quarter_bwd(0)
-    grad1(0)
     ring_start(0)
-    da_on(0)
+    jobs1[1]()
+    jobs1[2]()
+    arrived(dal.at[0:3], R.fi_r.at[3])
+    here(da, 0, R.ac_r)
 
     dq_all, dk_all, dv_all = R.q, R.k, R.v
 
     def attend_back(i):
-        da_i = da[i].reshape(BLK, width)
+        da_i = da_all[blk(i)]
         dc = dot_t(da_i, wo[...]).astype(bf16)
         q = R.q[blk(i)]
         k = R.k[blk(i)]
@@ -726,8 +769,7 @@
 
     def gin1(i):
         arrived(got1.at[i], R.rc_r.at[1, i])
-        mine = [dv1[part_at(b, i)].reshape(2, 16, width) for b in range(2)]
-        mine = jnp.stack(mine, axis=1).reshape(PIECE, width)
+        mine = dv1[piece_at(i)]
         for yy in range(2):
             has = jnp.where(y == yy, 1.0, 0.0).astype(f32)
             send2[i, yy] = (keep[i, yy].astype(f32) + got1[i, yy].astype(f32) + mine * has).astype(bf16)
@@ -743,13 +785,27 @@
 
     sent(send1, S_CORE0)
     sent(send2.at[:, 0], S_Y0)
-    for b in range(2):
-        arrived(da.at[:, 0:2, :, b], R.ac_r.at[b])
-
-    jobs1, jobs0, jobs2 = ring_jobs(1), ring_jobs(0), ring_jobs(2)
-    n_early = blocks
+    tile_row = lax.broadcasted_iota(jnp.int32, (16, 1), 0)
+    da_all = act
+
+    def late_rows(i):
+        da_all[blk(i)] = da[i].reshape(BLK, width)
+        for tt in range(4):
+            tile = dal[tt].astype(f32)
+            for k in range(2):
+                row = jnp.where(i >= slots, 0.0, tile[6:7]) if k == 0 else jnp.zeros((1, width), f32)
+                for b in range(blocks - slots):
+                    row = row + jnp.where(i == slots + b, tile[2 * b + k : 2 * b + k + 1], 0.0)
+                if k == 0:
+                    for s in range(1, slots):
+                        row = jnp.where(i == s, tile[6 + s : 7 + s], row)
+                at = pl.ds(pl.multiple_of(i * BLK + tt * PIECE + 32 * k, 16), 16)
+                old = da_all[at].astype(f32)
+                da_all[at] = (old + jnp.where(tile_row == 0, row, 0.0)).astype(bf16)
 
     def back_step(s):
+        at_step(s, {2: lambda: da_on(1), 3: lambda: here(da, 1, R.ac_r)})
+        late_rows(s)
         attend_back(s)
         rs0(1, s)
 
@@ -757,12 +813,8 @@
         def _():
             gin1(s - 1)
 
-        at_step(s, dict(enumerate(jobs1[:n_early])))
-        at_step(s, dict(enumerate(jobs0[:n_early])))
-
-        @pl.when(s >= 3)
-        def _():
-            gin2(s - 3)
+        at_step(s, dict(enumerate(jobs1[3 : 3 + blocks])))
+        at_step(s, dict(enumerate(jobs0[: blocks - 1], 1)))
 
     loop(blocks, back_step)
 
@@ -772,10 +824,14 @@
     cp(low_out, out.at[:, t], S_OUT, R.lo_r.at[0], ypeer).start()
     cp(low_out, out.at[:, t], S_OUT, R.lo_r.at[1], core).start()
 
+    late1, late0 = jobs1[3 + blocks :], jobs0[blocks - 1 :]
+    late = [job for pair in zip(late0, late1) for job in pair] + late0[len(late1) :]
+    late[0]()
+    late[1]()
     grads[2][0:local_width] = dot_l(dq_all[...], hid[...]).astype(bf16)
     grads[2][local_width : 2 * local_width] = dot_l(dk_all[...], hid[...]).astype(bf16)
     grads[2][2 * local_width : 3 * local_width] = dot_l(dv_all[...], hid[...]).astype(bf16)
-    grads[2][3 * local_width : 4 * local_width] = dot_l(R.ctx[...], da[...].reshape(rows, width)).astype(bf16)
+    grads[2][3 * local_width : 4 * local_width] = dot_l(R.ctx[...], da_all[...]).astype(bf16)
     ring_start(2)
 
     arrived(tsum.at[0:3], R.ts_r.at[0])
@@ -786,25 +842,28 @@
     vmail[dp] = sums[...].astype(bf16)
     loop(n_dp, lambda k: cp(vmail.at[dp], vmail.at[dp], S_VEC, R.dp_r.at[2], (dp_at(k), t)).start(), 1)
 
-    extra = [lambda: gin1(blocks - 1)] + [lambda i=i: gin2(i) for i in range(blocks - 3, blocks)]
-    late1, late0 = jobs1[n_early:], jobs0[n_early:]
-    for i in range(max(len(jobs2), len(late1), len(extra))):
-        for jobs in (late1, late0, jobs2, extra):
+    def vec_total():
+        arrived(vmail.at[1:], R.dp_r.at[2])
+        sums[...] = vmail[0].astype(f32)
+
+        def vec_add(n):
+            sums[...] += vmail[n].astype(f32)
+
+        loop(n_dp, vec_add, 1)
+        R.vec_out[...] = sums[...]
+        R.firsts_out[...] = firsts[...]
+
+    def out_on():
+        arrived(x1.at[:, 0], R.lo_r.at[0])
+        cp(out.at[:, t2], out.at[:, t2], S_OUT, R.lo_r.at[1], core).start()
+
+    extra = [lambda: gin1(blocks - 1)] + [lambda i=i: gin2(i) for i in range(blocks)] + [vec_total]
+    extra += [lambda: None, out_on]
+    for i in range(max(len(jobs2), len(late) - 2, len(extra))):
+        for jobs in (late[2:], jobs2, extra):
             if i < len(jobs):
                 jobs[i]()
 
-    arrived(vmail.at[1:], R.dp_r.at[2])
-    sums[...] = vmail[0].astype(f32)
-
-    def vec_add(n):
-        sums[...] += vmail[n].astype(f32)
-
-    loop(n_dp, vec_add, 1)
-    R.vec_out[...] = sums[...]
-    R.firsts_out[...] = firsts[...]
-    piece = x1.at[:, 0]
-    arrived(piece, R.lo_r.at[0])
-    cp(out.at[:, t2], out.at[:, t2], S_OUT, R.lo_r.at[1], core).start()
     arrived(x1.at[:, 0:2], R.lo_r.at[1])
     arrived(send1, R.go_r.at[0])
 
@@ -818,7 +877,8 @@
     sent(send2, S_Y1)
     for kind in (S_X1, S_DF, S_DA, S_OUT):
         sent(x1.at[:, 0:3], kind)
-    sent(firsts.at[0:3], S_FIRST)
+    sent(x1.at[0, 0:3], S_FIRST)
+    sent(dfl.at[0:3], S_PART)
     sent(mail.at[1:], S_MAIL)
     sent(vmail.at[1:], S_VEC)
     sent(tsum.at[0:3], S_TSUM)
@@ -850,7 +910,7 @@
         hid_in=any_, mask=vmem, bucket=smem, positive=smem, wqkv_in=any_, qv_bias=vmem, wo_in=any_, ob=vmem, g1=vmem,
         n1b=vmem, w1=any_, b1=vmem, w2=any_, fb=vmem, g2=vmem, n2b=vmem, upstream=any_,
     )
-    pieces = (blocks, 4, 2, 2, 16, width)
+    pieces = (blocks, 4, PIECE, width)
     pairs = (blocks, 2, PIECE, width)
     outs = dict(
         layer_out=(any_, pieces, bf16),
@@ -867,7 +927,7 @@
         wo=vm((local_width, width), bf16),
         wf1=vm((4, width, width), bf16),
         wf2=vm((4, width, width), bf16),
-        up=vm((blocks, 2, 2, 16, width), bf16),
+        up=vm((blocks, PIECE, width), bf16),
         bias1=vm((4, 8, width), f32),
         part=vm((BLK, width), f32),
         keep=vm(pairs, bf16),
@@ -881,20 +941,25 @@
         ctx=vm((rows, local_width), bf16),
         pb=vm((blocks, heads, BLK, BLK), bf16),
         x1=vm((blocks, 4, PIECE, width), bf16),
-        x1_own=vm((own, width), bf16),
+        x1f=vm((4, 16, width), bf16),
+        dfl=vm((4, 16, width), bf16),
+        dal=vm((4, 16, width), bf16),
+        parts=vm((4, 16, width), bf16),
+        parts_in=vm((4, 16, width), bf16),
+        act_late=vm((64, width), bf16),
+        du_late=vm((64, width), bf16),
         h1=vm((own, width), f32),
         n1=vm((own, width), f32),
         n2=vm((own, width), f32),
         rstd1=vm((own, 128), f32),
         rstd2=vm((own, 128), f32),
-        act=vm(pieces, bf16),
-        slope=vm(pieces, bf16),
+        act=vm((rows, width), bf16),
+        slope=vm((rows, width), bf16),
         wide=vm((own, width), f32),
         slope_own=vm((4, own, width), bf16),
-        low=vm((blocks, 2, 2, 16, width), bf16),
+        low=vm((blocks, PIECE, width), bf16),
         firsts=vm((4, 16, width), bf16),
         stage=vm((16, width), f32),
-        adds=vm((blocks, 8, width), f32),
         pack=vm((16, width // 2 + 128), f32),
         mail=vm((n_dp, 16, width // 2 + 128), bf16),
         qe=vm((32, width + 128), f32),
@@ -912,12 +977,12 @@
         ga3=vm((width, width), bf16),
         rb=vm((3, 2, RING - 1, share, width), bf16),
         load_sem=dma((6,)),
-        ss=dma((24,)),
+        ss=dma((25,)),
         wc_r=dma((1,)), wy_r=dma((2,)), wf_r=dma((2,)), wr_r=dma((2, 7)), bi_r=dma((1,)),
         rc_r=dma((2, blocks)), ry_r=dma((2, blocks)),
         gy_r=dma((blocks,)), gc_r=dma((blocks,)),
         fy_r=dma((2,)), fc_r=dma((2,)), ay_r=dma((2,)), ac_r=dma((2,)),
-        fi_r=dma((1,)), lo_r=dma((2,)), dp_r=dma((3,)), ts_r=dma((1,)),
+        fi_r=dma((5,)), lo_r=dma((2,)), dp_r=dma((3,)), ts_r=dma((1,)),
         rr_r=dma((3, 7)), rg_r=dma((3, 7)), go_r=dma((1,)),
     )
     if groups > 1:
@@ -943,7 +1008,7 @@
 
 def run_finish(lout, gin, o1, o2, o3, sums, firsts, slots, queries, local_width, n_dp):
     rows, width = lout.shape
-    steps = rows // BLK
+    steps = 3
     shapes = (
         ((rows, width), bf16), ((queries, width), bf16), ((2 * slots, width), bf16), ((1, 1), f32),
         ((rows, width), f32), ((3 * local_width, width), f32), ((2, local_width), f32), ((local_width, width), f32),
@@ -1008,7 +1073,7 @@
         hid_in=hidden_in, mask=token_mask, bucket=bucket, positive=positive, wqkv_in=qkv_weight.transpose(0, 2, 1),
         qv_bias=qv_bias, wo_in=out_weight, ob=out_bias, g1=norm1_gain, n1b=norm1_bias, w1=ffn_in, b1=ffn_in_bias,
         w2=ffn_out, fb=ffn_out_bias, g2=norm2_gain, n2b=norm2_bias,
-        upstream=upstream.reshape(blocks, 4, 2, 2, 16, width),
+        upstream=upstream.reshape(blocks, 4, PIECE, width),
     )
     lout, gin, o1, o2, o3, sums, firsts = run_layer(n_dp, ins, (rows, width, slots, queries, local_width))
     lout, gin = lout.reshape(rows, width), gin.reshape(rows, width)

time: 167 us -> 159 us (0.952)
  Pallas kernels: 166 us -> 158 us
    pallas_call x1, Pallas kernels: 157 us -> 149 us  [run_layer(): pl.pallas_call(kernel, name='layer', out_shape=[jax.ShapeDtypeStruct(shap...]
where the time goes in v3:
time: 159 us
  Pallas kernels  158 us (99%)
    pallas_call x1, Pallas kernels, run_layer(): pl.pallas_call(kernel, name='layer', out_shape=[jax.ShapeDtypeStruct(shap...  149 us
    pallas_call x1, Pallas kernels, run_finish(): pl.pallas_call(kernel, name='finish', grid=(steps,), out_shape=[jax.Shape...  8.81 us

profile of v3, /device:TPU:0, one launch (start us, length us, event | category | flops | bytes accessed | tf_op | source)
XLA Modules:
  0.0 158.8 jit_solution(7947554521686343192)
XLA Ops:
  0.7 149.2 %layer.1 = (bf16[6,4,64,768]{3,2,1,0:T(8,128)(2,1)}, bf16[6,4,64,768]{3,2,1,0:T(8,128)(2,1)}, bf16[768,768]{1,0:T(8,128)(2,1)}, bf16[768,768]{1,0:T(8,128)(2,1)}...) custom-call(bf16[1536,768]{1,0:T(8,128)(2,1)} %refs_0_.1, s32[1536]{0:T(1024)} %refs_1_.1, ...), custom_call_target="tpu_custom_call" | custom-call | tf_op jit(solution)/shard_map/layer/pallas_call | solution.py:996
  149.8 8.8 %finish.1 = (bf16[1536,768]{1,0:T(8,128)(2,1)}, bf16[24,768]{1,0:T(8,128)(2,1)}, bf16[6,768]{1,0:T(8,128)(2,1)}, f32[1,1]{1,0:T(1,128)}, f32[1536,768]{1,0:T(8,1...) custom-call(bf16[1536,768]{1,0:T(8,128)(2,1)} %bitcast.9, ...), custom_call_target="tpu_custom_call" | custom-call | tf_op jit(solution)/shard_map/finish/pallas_call | solution.py:1049

commit v4 on v3

--- a/solution.py
+++ b/solution.py
@@ -80,7 +80,7 @@
         return lax.rem(dp + k, n_dp)
 
     (S_SHARE, S_WCORE, S_WRING, S_WON, S_BIAS, S_CORE0, S_Y0, S_CORE1, S_Y1, S_X1, S_FIRST, S_DF, S_DA, S_OUT, S_MAIL,
-     S_BACK, S_VEC, S_TSUM, S_RING, S_GATHER, S_LOCAL, S_GLOCAL, S_GCORE, S_OUTL, S_PART) = range(25)
+     S_BACK, S_VEC, S_TSUM, S_RING, S_GATHER, S_LOCAL, S_GLOCAL, S_GCORE, S_OUTL, S_PART, S_VSHARE) = range(26)
 
     def cp(src, dst, kind, rsem, dev):
         return pltpu.make_async_remote_copy(
@@ -290,6 +290,7 @@
         rstd1[piece_at(i)] = jnp.broadcast_to(rstd, (PIECE, 128))
         h1[piece_at(i)] = out
         x1[i, t] = out.astype(bf16)
+        ag0(x1.at[i, t], S_X1, R.gy_r.at[i], R.gc_r.at[i])
 
     def at_step(s, jobs):
         for i, job in jobs.items():
@@ -324,9 +325,6 @@
         at_step(s, {0: wb[1], 1: wa[4], 2: both(wb[2], wa[5]), 3: wb[3], 4: both(wa[6], wb[4]), 5: wa[7]})
 
     loop(blocks, norm_step)
-    def x1_out(i):
-        ag0(x1.at[i, t], S_X1, R.gy_r.at[i], R.gc_r.at[i])
-
     x1f = R.x1f
     x1f[t] = pick(h1).astype(bf16)
 
@@ -335,7 +333,6 @@
             cp(tiles.at[t], tiles.at[t], S_FIRST, R.fi_r.at[which], mate).start()
 
     tile_out(x1f, 1)
-    loop(blocks - 2, x1_out)
 
     for one in loads[3:]:
         one.wait()
@@ -378,14 +375,14 @@
     def own_step(s):
         own_in(s)
         at_step(
-            s, {0: wb[5], 1: both(wb[6], lambda: arrived(R.wf1.at[0], R.wf_r.at[0])), 2: wb[7]}
+            s, {0: wb[5], 2: both(wb[6], lambda: arrived(R.wf1.at[0], R.wf_r.at[0]))}
         )
 
     loop(4, own_step)
     wide[...] = jnp.zeros((own, width), f32)
 
     def out_step(s):
-        at_step(s, {3: lambda: arrived(R.wf2.at[0], R.wf_r.at[1])})
+        at_step(s, {2: wb[7], 3: lambda: arrived(R.wf2.at[0], R.wf_r.at[1])})
         own_out(s)
 
     loop(4, out_step)
@@ -407,7 +404,6 @@
     stage[...] = jnp.zeros((16, width), f32)
     firsts[t] = pick(h1).astype(bf16)
     tile_out(firsts, 0)
-    loop(blocks, x1_out, blocks - 2)
 
     sums = R.sums
     sums[...] = jnp.zeros((16, width), f32)
@@ -813,8 +809,8 @@
         def _():
             gin1(s - 1)
 
-        at_step(s, dict(enumerate(jobs1[3 : 3 + blocks])))
-        at_step(s, dict(enumerate(jobs0[: blocks - 1], 1)))
+        at_step(s, {1: both(jobs1[3]), 2: both(jobs1[4]), 3: both(jobs1[5]), 4: both(jobs1[6]), 5: both(jobs1[7])})
+        at_step(s, {1: both(jobs0[0]), 2: both(jobs0[1]), 3: both(jobs0[2]), 4: both(jobs0[3]), 5: both(jobs0[4])})
 
     loop(blocks, back_step)
 
@@ -824,10 +820,8 @@
     cp(low_out, out.at[:, t], S_OUT, R.lo_r.at[0], ypeer).start()
     cp(low_out, out.at[:, t], S_OUT, R.lo_r.at[1], core).start()
 
-    late1, late0 = jobs1[3 + blocks :], jobs0[blocks - 1 :]
+    late1, late0 = jobs1[8:], jobs0[5:]
     late = [job for pair in zip(late0, late1) for job in pair] + late0[len(late1) :]
-    late[0]()
-    late[1]()
     grads[2][0:local_width] = dot_l(dq_all[...], hid[...]).astype(bf16)
     grads[2][local_width : 2 * local_width] = dot_l(dk_all[...], hid[...]).astype(bf16)
     grads[2][2 * local_width : 3 * local_width] = dot_l(dv_all[...], hid[...]).astype(bf16)
@@ -839,18 +833,43 @@
     loss_low = sums[6:7].astype(bf16).astype(f32)
     sums[7:8] = sums[6:7] - loss_low
     vmail = R.vmail
-    vmail[dp] = sums[...].astype(bf16)
+    vpack = R.vpack
+    third = width // 3
+    vpack[...] = jnp.zeros((16, third), f32)
+    for j in range(2):
+        row = jnp.zeros((1, width), f32)
+        for tt in range(4):
+            row = row + jnp.where(t == tt, sums[2 * tt + j : 2 * tt + j + 1], 0.0)
+        for p in range(3):
+            vpack[3 * j + p : 3 * j + p + 1] = row[:, p * third : (p + 1) * third]
+    for p in range(3):
+        vpack[6 + p : 7 + p] = sums[8:9, p * third : (p + 1) * third]
+    vpack[9:11] = sums[9:11, 0:third]
+    vmail[dp] = vpack[...].astype(bf16)
     loop(n_dp, lambda k: cp(vmail.at[dp], vmail.at[dp], S_VEC, R.dp_r.at[2], (dp_at(k), t)).start(), 1)
 
     def vec_total():
         arrived(vmail.at[1:], R.dp_r.at[2])
-        sums[...] = vmail[0].astype(f32)
+        vpack[...] = vmail[0].astype(f32)
 
         def vec_add(n):
-            sums[...] += vmail[n].astype(f32)
+            vpack[...] += vmail[n].astype(f32)
 
         loop(n_dp, vec_add, 1)
-        R.vec_out[...] = sums[...]
+        R.vshare[t] = vpack[0:8]
+        for mate in mates:
+            cp(R.vshare.at[t], R.vshare.at[t], S_VSHARE, R.vs_r.at[0], mate).start()
+
+    def vec_out():
+        arrived(R.vshare.at[0:3], R.vs_r.at[0])
+        R.vec_out[...] = jnp.zeros((16, width), f32)
+        for p in range(3):
+            at = slice(p * third, (p + 1) * third)
+            for tt in range(4):
+                for j in range(2):
+                    R.vec_out[2 * tt + j : 2 * tt + j + 1, at] = R.vshare[tt, 3 * j + p : 3 * j + p + 1]
+            R.vec_out[8:9, at] = vpack[6 + p : 7 + p]
+        R.vec_out[9:11, 0:third] = vpack[9:11]
         R.firsts_out[...] = firsts[...]
 
     def out_on():
@@ -858,9 +877,9 @@
         cp(out.at[:, t2], out.at[:, t2], S_OUT, R.lo_r.at[1], core).start()
 
     extra = [lambda: gin1(blocks - 1)] + [lambda i=i: gin2(i) for i in range(blocks)] + [vec_total]
-    extra += [lambda: None, out_on]
-    for i in range(max(len(jobs2), len(late) - 2, len(extra))):
-        for jobs in (late[2:], jobs2, extra):
+    extra += [lambda: None, out_on, vec_out]
+    for i in range(max(len(jobs2), len(late), len(extra))):
+        for jobs in (late, jobs2, extra):
             if i < len(jobs):
                 jobs[i]()
 
@@ -881,6 +900,7 @@
     sent(dfl.at[0:3], S_PART)
     sent(mail.at[1:], S_MAIL)
     sent(vmail.at[1:], S_VEC)
+    sent(R.vshare.at[0:3], S_VSHARE)
     sent(tsum.at[0:3], S_TSUM)
 
     @pl.when(c == 0)
@@ -969,7 +989,9 @@
         back=vm((n_dp, 8, width), f32),
         sums=vm((16, width), f32),
         tsum=vm((4, 8, width), f32),
-        vmail=vm((n_dp, 16, width), bf16),
+        vmail=vm((n_dp, 16, width // 3), bf16),
+        vpack=vm((16, width // 3), f32),
+        vshare=vm((4, 8, width // 3), f32),
         df=vm(pieces, bf16),
         da=vm(pieces, bf16),
         ga1=vm((width, width), bf16),
@@ -977,12 +999,12 @@
         ga3=vm((width, width), bf16),
         rb=vm((3, 2, RING - 1, share, width), bf16),
         load_sem=dma((6,)),
-        ss=dma((25,)),
+        ss=dma((26,)),
         wc_r=dma((1,)), wy_r=dma((2,)), wf_r=dma((2,)), wr_r=dma((2, 7)), bi_r=dma((1,)),
         rc_r=dma((2, blocks)), ry_r=dma((2, blocks)),
         gy_r=dma((blocks,)), gc_r=dma((blocks,)),
         fy_r=dma((2,)), fc_r=dma((2,)), ay_r=dma((2,)), ac_r=dma((2,)),
-        fi_r=dma((5,)), lo_r=dma((2,)), dp_r=dma((3,)), ts_r=dma((1,)),
+        fi_r=dma((5,)), vs_r=dma((1,)), lo_r=dma((2,)), dp_r=dma((3,)), ts_r=dma((1,)),
         rr_r=dma((3, 7)), rg_r=dma((3, 7)), go_r=dma((1,)),
     )
     if groups > 1:
@@ -1008,7 +1030,7 @@
 
 def run_finish(lout, gin, o1, o2, o3, sums, firsts, slots, queries, local_width, n_dp):
     rows, width = lout.shape
-    steps = 3
+    steps = 2
     shapes = (
         ((rows, width), bf16), ((queries, width), bf16), ((2 * slots, width), bf16), ((1, 1), f32),
         ((rows, width), f32), ((3 * local_width, width), f32), ((2, local_width), f32), ((local_width, width), f32),

time: 159 us -> 149 us (0.937)
  Pallas kernels: 158 us -> 148 us
    pallas_call x1, Pallas kernels: 149 us -> 140 us  [run_layer(): pl.pallas_call(kernel, name='layer', out_shape=[jax.ShapeDtypeStruct(shap...]
where the time goes in v4:
time: 149 us
  Pallas kernels  148 us (99%)
    pallas_call x1, Pallas kernels, run_layer(): pl.pallas_call(kernel, name='layer', out_shape=[jax.ShapeDtypeStruct(shap...  140 us
    pallas_call x1, Pallas kernels, run_finish(): pl.pallas_call(kernel, name='finish', grid=(steps,), out_shape=[jax.Shape...  7.8 us

profile of v4, /device:TPU:0, one launch (start us, length us, event | category | flops | bytes accessed | tf_op | source)
XLA Modules:
  0.0 148.9 jit_solution(155214772908954600)
XLA Ops:
  0.7 140.3 %layer.1 = (bf16[6,4,64,768]{3,2,1,0:T(8,128)(2,1)}, bf16[6,4,64,768]{3,2,1,0:T(8,128)(2,1)}, bf16[768,768]{1,0:T(8,128)(2,1)}, bf16[768,768]{1,0:T(8,128)(2,1)}...) custom-call(bf16[1536,768]{1,0:T(8,128)(2,1)} %refs_0_.1, s32[1536]{0:T(1024)} %refs_1_.1, ...), custom_call_target="tpu_custom_call" | custom-call | tf_op jit(solution)/shard_map/layer/pallas_call | solution.py:1018
  140.9 7.8 %finish.1 = (bf16[1536,768]{1,0:T(8,128)(2,1)}, bf16[24,768]{1,0:T(8,128)(2,1)}, bf16[6,768]{1,0:T(8,128)(2,1)}, f32[1,1]{1,0:T(1,128)}, f32[1536,768]{1,0:T(8,1...) custom-call(bf16[1536,768]{1,0:T(8,128)(2,1)} %bitcast.9, ...), custom_call_target="tpu_custom_call" | custom-call | tf_op jit(solution)/shard_map/finish/pallas_call | solution.py:1071

commit v5 on v4

--- a/solution.py
+++ b/solution.py
@@ -879,7 +879,7 @@
     extra = [lambda: gin1(blocks - 1)] + [lambda i=i: gin2(i) for i in range(blocks)] + [vec_total]
     extra += [lambda: None, out_on, vec_out]
     for i in range(max(len(jobs2), len(late), len(extra))):
-        for jobs in (late, jobs2, extra):
+        for jobs in (jobs2, late, extra):
             if i < len(jobs):
                 jobs[i]()
 

time: 149 us -> 149 us (level)
  no operation moved by 1% of the time
where the time goes in v5:
time: 149 us; the launch traced here: 148 us
  Pallas kernels  148 us (99%)
    pallas_call x1, Pallas kernels, run_layer(): pl.pallas_call(kernel, name='layer', out_shape=[jax.ShapeDtypeStruct(shap...  140 us
    pallas_call x1, Pallas kernels, run_finish(): pl.pallas_call(kernel, name='finish', grid=(steps,), out_shape=[jax.Shape...  7.8 us

profile of v5, /device:TPU:0, one launch (start us, length us, event | category | flops | bytes accessed | tf_op | source)
XLA Modules:
  0.0 148.4 jit_solution(6220175865589029857)
XLA Ops:
  0.7 139.8 %layer.1 = (bf16[6,4,64,768]{3,2,1,0:T(8,128)(2,1)}, bf16[6,4,64,768]{3,2,1,0:T(8,128)(2,1)}, bf16[768,768]{1,0:T(8,128)(2,1)}, bf16[768,768]{1,0:T(8,128)(2,1)}...) custom-call(bf16[1536,768]{1,0:T(8,128)(2,1)} %refs_0_.1, s32[1536]{0:T(1024)} %refs_1_.1, ...), custom_call_target="tpu_custom_call" | custom-call | tf_op jit(solution)/shard_map/layer/pallas_call | solution.py:1018
  140.5 7.8 %finish.1 = (bf16[1536,768]{1,0:T(8,128)(2,1)}, bf16[24,768]{1,0:T(8,128)(2,1)}, bf16[6,768]{1,0:T(8,128)(2,1)}, f32[1,1]{1,0:T(1,128)}, f32[1536,768]{1,0:T(8,1...) custom-call(bf16[1536,768]{1,0:T(8,128)(2,1)} %bitcast.9, ...), custom_call_target="tpu_custom_call" | custom-call | tf_op jit(solution)/shard_map/finish/pallas_call | solution.py:1071
